TPU v7x, 128 devices: a whole 4x4x4 slice. The times are simulated.
128 devices in a mesh: lat: 4 (over z), lon: 32 (over x, y, core).
Axes of the slice: x: 4, y: 4, z: 4, core: 2. Of those that a mesh axis runs over, the one named last changes fastest.
Arguments:
- fields: bfloat16 [4, 69, 96, 4096], P(None, None, 'lat', 'lon'), may hold values from -6 to 6
- conv_weight: bfloat16 [9, 128, 69], replicated, may hold values from -0.25 to 0.25
- kv_weight: bfloat16 [512, 128], replicated, may hold values from -0.5 to 0.5
- out_weight: bfloat16 [256, 256], replicated, may hold values from -0.375 to 0.375
- norm_gain: float32 [256], replicated, may hold values from 0.5 to 1.5
- queries: bfloat16 [256, 256], replicated, may hold values from -64 to 64
Outputs:
- features: bfloat16 [4, 128, 96, 4096], P(None, None, 'lat', 'lon')
- latents: float32 [4, 256, 256], replicated
All inputs are finite; a program needn't handle non-finite values.
Results may differ from a plain program's by a relative error of at most 0.0035.
The roundings to bfloat16 on the way count: a program that leaves them out, or rounds other values in their place, can miss the bound.
Values may be sent and summed in bfloat16 or wider, within the bound.
A program may use at most 320 MiB of HBM per device.

v0:
```python
import jax
import jax.numpy as jnp
from jax import lax
from jax.sharding import PartitionSpec as P

DL = 256
Q = 256
HEADS = 4
HD = 64
BLK = 8


def extended(block, sides, width, periodic):
    for axis, dim in sides:
        count = lax.axis_size(axis)
        forward = [(i, i + 1) for i in range(count - 1)]
        if periodic:
            forward.append((count - 1, 0))
        backward = [(target, source) for source, target in forward]
        low = lax.ppermute(
            lax.slice_in_dim(block, block.shape[dim] - width, None, axis=dim), axis, forward
        )
        high = lax.ppermute(lax.slice_in_dim(block, 0, width, axis=dim), axis, backward)
        block = jnp.concatenate([low, block, high], axis=dim)
    return block


def convolve_block(window_in, conv_weight, lat_rows, lon_cols):
    running = jnp.zeros((window_in.shape[0], conv_weight.shape[1], lat_rows, lon_cols), jnp.float32)
    for tap_index in range(9):
        row_off = tap_index // 3
        col_off = tap_index % 3
        piece = window_in[:, :, row_off : row_off + lat_rows, col_off : col_off + lon_cols]
        running = running + jnp.einsum(
            "fc,bcin->bfin", conv_weight[tap_index], piece, preferred_element_type=jnp.float32
        )
    return running


def block_terms(window_in, conv_weight, kv_weight, queries, lat_rows, lon_cols):
    samples = window_in.shape[0]
    convolved = convolve_block(window_in, conv_weight, lat_rows, lon_cols)
    block_features = jax.nn.gelu(convolved, approximate=True).astype(jnp.bfloat16)
    flattened = block_features.reshape(samples, block_features.shape[1], lat_rows * lon_cols)
    key_value = jnp.einsum(
        "of,bfn->bon", kv_weight, flattened, preferred_element_type=jnp.float32
    ).astype(jnp.bfloat16)
    key_heads = key_value[:, :DL].reshape(samples, HEADS, HD, lat_rows * lon_cols)
    value_heads = key_value[:, DL:].reshape(samples, HEADS, HD, lat_rows * lon_cols)
    query_heads = queries.reshape(Q, HEADS, HD)
    scores = jnp.einsum(
        "qhd,bhdn->bhqn", query_heads, key_heads, preferred_element_type=jnp.float32
    ) * HD ** (-0.5)
    maxima = jnp.max(scores, axis=-1)
    exponent = jnp.exp(scores - maxima[..., None])
    totals = jnp.sum(exponent, axis=-1)
    weights_bf = exponent.astype(jnp.bfloat16)
    weighted = jnp.einsum(
        "bhqn,bhdn->bqhd", weights_bf, value_heads, preferred_element_type=jnp.float32
    )
    return (block_features, maxima, totals, weighted.reshape(samples, Q, DL))


def rescale(weighted, factor):
    full_shape = weighted.shape
    heads_view = weighted.reshape(full_shape[0], full_shape[1], factor.shape[1], -1)
    return (heads_view * jnp.transpose(factor, (0, 2, 1))[..., None]).reshape(full_shape)


def normalize(weighted, totals):
    full_shape = weighted.shape
    heads_view = weighted.reshape(full_shape[0], full_shape[1], totals.shape[1], -1)
    return (heads_view / jnp.transpose(totals, (0, 2, 1))[..., None]).reshape(full_shape)


def combine_partial(earlier, later):
    highest = jnp.maximum(earlier[0], later[0])
    scale_one = jnp.exp(earlier[0] - highest)
    scale_two = jnp.exp(later[0] - highest)
    totals = earlier[1] * scale_one + later[1] * scale_two
    weighted = rescale(earlier[2], scale_one) + rescale(later[2], scale_two)
    return (highest, totals, weighted)


def per_device(fields, conv_weight, kv_weight, out_weight, norm_gain, queries):
    samples, channels, lat_rows, lon_cols = fields.shape
    widened = extended(fields, (("lon", 3),), 1, True)
    padded = extended(widened, (("lat", 2),), 1, False)
    block_count = lat_rows // BLK
    initial = (
        jnp.full((samples, HEADS, Q), -1e30, jnp.float32),
        jnp.zeros((samples, HEADS, Q), jnp.float32),
        jnp.zeros((samples, Q, DL), jnp.float32),
    )

    def scan_step(running_state, block_index):
        zero_index = jnp.zeros((), jnp.int32)
        window_in = lax.dynamic_slice(
            padded,
            (zero_index, zero_index, block_index * BLK, zero_index),
            (samples, channels, BLK + 2, lon_cols + 2),
        )
        block_features, maxima, totals, weighted = block_terms(
            window_in, conv_weight, kv_weight, queries, BLK, lon_cols
        )
        return (combine_partial(running_state, (maxima, totals, weighted)), block_features)

    running_state, feats = lax.scan(scan_step, initial, jnp.arange(block_count, dtype=jnp.int32))
    features = jnp.transpose(feats, (1, 2, 0, 3, 4)).reshape(
        samples, feats.shape[2], lat_rows, lon_cols
    )
    maxima, totals, weighted = running_state
    peak = lax.pmax(maxima, ("lat", "lon"))
    factor = jnp.exp(maxima - peak)
    total_all, weighted_all = lax.psum((totals * factor, rescale(weighted, factor)), ("lat", "lon"))
    attended = normalize(weighted_all, total_all).astype(jnp.bfloat16)
    projected = jnp.einsum("bqe,ef->bqf", attended, out_weight, preferred_element_type=jnp.float32)
    latents = (
        projected
        * lax.rsqrt(jnp.mean(projected * projected, axis=-1, keepdims=True) + 1e-06)
        * norm_gain
    )
    return (features, latents)


def solution(mesh):
    in_specs = (P(None, None, "lat", "lon"), P(), P(), P(), P(), P())
    out_specs = (P(None, None, "lat", "lon"), P())
    return jax.shard_map(
        per_device, mesh=mesh, in_specs=in_specs, out_specs=out_specs, check_vma=False
    )
```

profile of v0, /device:TPU:1, one launch (start us, length us, event | category | flops | bytes accessed | tf_op | source)
XLA Modules:
  0.0 357.0 jit_solution(6077732282394592555)
XLA Ops:
  7.2 4.0 %fusion.74 = (bf16[4,69,24,1]{3,2,1,0:T(8,128)(2,1)}, bf16[4,69,24,1]{3,2,1,0:T(8,128)(2,1)S(1)}) fusion(bf16[4,69,24,128]{3,2,1,0:T(8,128)(2,1)} %param.8), kind=kLoop, calls=%fused_computation.92 | loop fusion | bytes 52992 | tf_op jit(solution)/shard_map/slice | solution.py:21
  11.2 2.2 copy.56
  13.4 2.8 collective-permute-start
  16.2 1.2 copy.57
  17.4 1.7 copy.31
  19.1 1.9 copy.30
  21.0 1.9 copy.32
  22.9 1.2 pad_maximum_fusion.3
  24.1 4.2 %collective-permute-start.2 = (bf16[4,69,1,130]{3,1,2,0:T(8,128)(2,1)S(1)}, bf16[4,69,1,130]{3,1,2,0:T(8,128)(2,1)}, u32[]{:S(2)}, u32[]{:S(2)}) collective-permute-start(bf16[4,69,1,130]{3,1,2,0:T(8,128)(2,1)S(1)} %get-tuple-element.150), channel_id=1, source_target_pairs={{0,32},{32,64},{64,96},{1,33},{33,65},{65,97},{2,34},{34,66},{66,9... | collective-permute-start | bytes 215288 | tf_op jit(solution)/shard_map/ppermute | solution.py:20
  28.3 1.3 collective-permute-start.3
  29.8 4.5 %collective-permute-done.3 = bf16[4,69,1,130]{3,1,2,0:T(8,128)(2,1)} collective-permute-done((bf16[4,69,1,130]{3,1,2,0:T(8,128)(2,1)S(1)}, bf16[4,69,1,130]{3,1,2,0:T(8,128)(2,1)}, u32[]{:S(2)}, u32[]{:S(2)}) %collective-permute-start.3) | collective-permute-done | bytes 71792 | tf_op jit(solution)/shard_map/ppermute | solution.py:23
  34.3 5.1 %pad_maximum_fusion = bf16[4,69,26,130]{3,1,2,0:T(8,128)(2,1)} fusion(bf16[4,69,1,130]{3,1,2,0:T(8,128)(2,1)} %collective-permute-done.3, bf16[4,69,24,1]{3,1,2,0:T(8,128)(2,1)} %copy.32, bf16[4,69,24,128]{3,1,2,0:T(8,128)(2,1)S(1)} %copy.31, bf16[4,69,24,1]{3,1,2,0:T(8,128)(2,1)} %copy.30, bf16[4,69,1,130]{3,1,2,0:T(8,128)(2,1)} %collective-permute-done.2), kind=kLoop, calls=%fused_computation.76 | loop fusion | flops 9328800 | bytes 3731520 | tf_op jit(solution)/shard_map/concatenate | solution.py:24
  39.5 92.3 %while.17 = (s32[]{:T(128)}, f32[4,4,256]{2,0,1:T(4,128)}, f32[4,4,256]{2,0,1:T(4,128)}, f32[4,256,256]{1,2,0:T(8,128)S(1)}, bf16[3,4,128,8,128]{2,4,3,1,0:T(8,1...) while((s32[]{:T(128)}, f32[4,4,256]{2,0,1:T(4,128)}, ...), condition=%wide.region_3.4_spmd.clone, body=%wide.region_0.3_spmd.clone.sunk | while | flops 2299035648 | bytes 122200216 | solution.py:108
  39.7 0.6 dynamic_slice.10
  40.9 2.0 fusion.134
  42.9 2.1 fusion.136
  45.1 2.0 fusion.137
  48.1 0.7 fusion.139
  48.9 0.7 fusion.141
  49.6 0.5 fusion.140
  50.1 2.8 bitcast_dynamic-update-slice_fusion.2
  52.9 1.3 convert_bitcast_fusion.2
  54.6 2.4 bitcast_reduce_fusion.2
  57.0 5.7 %fusion.144 = (bf16[4,4,256,1024]{2,3,0,1:T(8,128)(2,1)}, f32[4,4,256]{2,0,1:T(4,128)}) fusion(f32[4,4,1024,256]{3,2,1,0:T(8,128)S(1)} %get-tuple-element.235, f32[4,4,256]{2,0,1:T(4,128)S(1)} %get-tuple-element.233), kind=kLoop, calls=%fused_computation.3.clone.1 | loop fusion | flops 16773120 | bytes 25198592 | tf_op jit(solution)/shard_map/while/body/eval_jaxpr/convert_element_type | solution.py:57
  62.8 1.4 fusion.145
  64.1 4.8 %fusion.146 = f32[4,256,4,64]{1,3,2,0:T(8,128)S(1)} fusion(bf16[4,4,64,1024]{3,2,1,0:T(8,128)(2,1)S(1)} %bitcast.183, bf16[4,4,256,1024]{2,3,0,1:T(8,128)(2,1)} %get-tuple-element.239, f32[4,256,4]{1,2,0:T(4,128)S(1)} %copy.74), kind=kOutput, calls=%fused_computation.20.clone.1 | convolution fusion | flops 537133056 | bytes 11550720 | tf_op jit(solution)/shard_map/while/body/eval_jaxpr/bhqn,bhdn->bqhd/dot_general | solution.py:58
  69.3 0.6 copy.88
  69.9 0.6 dynamic_slice.10
  71.2 2.0 fusion.134
  73.2 2.1 fusion.136
  75.3 2.0 fusion.137
  78.4 0.7 fusion.139
  79.1 0.7 fusion.141
  80.3 2.8 bitcast_dynamic-update-slice_fusion.2
  83.1 1.3 convert_bitcast_fusion.2
  84.8 2.4 bitcast_reduce_fusion.2
  87.2 5.7 %fusion.144 = (bf16[4,4,256,1024]{2,3,0,1:T(8,128)(2,1)}, f32[4,4,256]{2,0,1:T(4,128)}) fusion(f32[4,4,1024,256]{3,2,1,0:T(8,128)S(1)} %get-tuple-element.235, f32[4,4,256]{2,0,1:T(4,128)S(1)} %get-tuple-element.233), kind=kLoop, calls=%fused_computation.3.clone.1 | loop fusion | flops 16773120 | bytes 25198592 | tf_op jit(solution)/shard_map/while/body/eval_jaxpr/convert_element_type | solution.py:57
  93.0 0.7 fusion.143
  93.7 1.4 fusion.145
  95.1 4.8 %fusion.146 = f32[4,256,4,64]{1,3,2,0:T(8,128)S(1)} fusion(bf16[4,4,64,1024]{3,2,1,0:T(8,128)(2,1)S(1)} %bitcast.183, bf16[4,4,256,1024]{2,3,0,1:T(8,128)(2,1)} %get-tuple-element.239, f32[4,256,4]{1,2,0:T(4,128)S(1)} %copy.74), kind=kOutput, calls=%fused_computation.20.clone.1 | convolution fusion | flops 537133056 | bytes 11550720 | tf_op jit(solution)/shard_map/while/body/eval_jaxpr/bhqn,bhdn->bqhd/dot_general | solution.py:58
  100.2 0.6 copy.88
  100.8 0.6 dynamic_slice.10
  102.1 2.0 fusion.134
  104.1 2.1 fusion.136
  106.3 2.0 fusion.137
  109.3 0.7 fusion.139
  110.0 0.7 fusion.141
  110.8 0.5 fusion.140
  111.3 2.7 bitcast_dynamic-update-slice_fusion.2
  114.0 1.3 convert_bitcast_fusion.2
  115.7 2.4 bitcast_reduce_fusion.2
  118.1 5.7 %fusion.144 = (bf16[4,4,256,1024]{2,3,0,1:T(8,128)(2,1)}, f32[4,4,256]{2,0,1:T(4,128)}) fusion(f32[4,4,1024,256]{3,2,1,0:T(8,128)S(1)} %get-tuple-element.235, f32[4,4,256]{2,0,1:T(4,128)S(1)} %get-tuple-element.233), kind=kLoop, calls=%fused_computation.3.clone.1 | loop fusion | flops 16773120 | bytes 25198592 | tf_op jit(solution)/shard_map/while/body/eval_jaxpr/convert_element_type | solution.py:57
  123.9 0.7 fusion.143
  124.6 1.4 fusion.145
  126.0 4.8 %fusion.146 = f32[4,256,4,64]{1,3,2,0:T(8,128)S(1)} fusion(bf16[4,4,64,1024]{3,2,1,0:T(8,128)(2,1)S(1)} %bitcast.183, bf16[4,4,256,1024]{2,3,0,1:T(8,128)(2,1)} %get-tuple-element.239, f32[4,256,4]{1,2,0:T(4,128)S(1)} %copy.74), kind=kOutput, calls=%fused_computation.20.clone.1 | convolution fusion | flops 537133056 | bytes 11550720 | tf_op jit(solution)/shard_map/while/body/eval_jaxpr/bhqn,bhdn->bqhd/dot_general | solution.py:58
  131.2 0.6 copy.88
  131.8 68.2 %pmax.7 = f32[4,4,256]{2,0,1:T(4,128)S(1)} all-reduce(f32[4,4,256]{2,0,1:T(4,128)} %get-tuple-element.59), channel_id=1, replica_groups=mesh['lat'=4,'lon'=32] {'lat','lon'}, use_global_device_ids=true, to_apply=%region_4.5 | all-reduce | flops 4096 | bytes 32768 | tf_op jit(solution)/shard_map/pmax | solution.py:113
  200.0 0.7 multiply_bitcast_fusion
  200.7 1.0 bitcast_multiply_fusion.1
  201.8 63.9 %psum.15 = f32[4,256,4]{1,0,2:T(4,128)S(1)} all-reduce(f32[4,256,4]{1,0,2:T(4,128)S(1)} %get-tuple-element.154), channel_id=1, replica_groups=mesh['lat'=4,'lon'=32] {'lat','lon'}, use_global_device_ids=true, to_apply=%region_6.7 | all-reduce | flops 4096 | bytes 32768 | tf_op jit(solution)/shard_map/psum | solution.py:115
  265.8 4.8 %copy.34 = bf16[4,128,3,8,128]{4,3,2,1,0:T(8,128)(2,1)} copy(bf16[4,128,3,8,128]{1,4,3,0,2:T(8,128)(2,1)} %bitcast.185) | data formatting | bytes 6291456 | tf_op jit(solution)/shard_map/transpose | solution.py:109
  270.6 76.4 %all-reduce.2.cloned.1.call-done = f32[4,256,256]{1,2,0:T(8,128)} async-done(((f32[4,256,256]{1,2,0:T(8,128)}), f32[4,256,256]{1,2,0:T(8,128)}) %all-reduce.2.cloned.1.call-update) | async-done | bytes 1048592 | tf_op jit(solution)/shard_map/psum | solution.py:115
  347.0 1.3 fusion.69
  348.8 1.3 copy.39
  (69 shorter events, 6.8 us)
Async XLA Ops:
  7.2 341.1 %copy-start = (bf16[256,256]{1,0:T(8,128)(2,1)S(1)}, bf16[256,256]{1,0:T(8,128)(2,1)}, u32[]{:S(2)}) copy-start(bf16[256,256]{1,0:T(8,128)(2,1)} %param.11) | copy-start | bytes 393220
  7.2 339.8 %all-reduce.2.cloned.1.call-start = ((), (), s32[]{:S(2)}) async-start(), calls=%async_computation | async-start | bytes 2097152 | tf_op jit(solution)/shard_map/psum | solution.py:115
  13.4 5.7 %collective-permute-start = (bf16[4,69,24,1]{1,2,3,0:T(8,128)(2,1)S(1)}, bf16[4,69,24,1]{1,2,3,0:T(8,128)(2,1)S(1)}, u32[]{:S(2)}, u32[]{:S(2)}) collective-permute-start(bf16[4,69,24,1]{1,2,3,0:T(8,128)(2,1)S(1)} %copy.56), channel_id=1, source_target_pairs={{0,1},{1,2},{2,3},{3,4},{4,5},{5,6},{6,7},{7,8},{8,9},{9,10},{10,1... | collective-permute-start | bytes 39752 | tf_op jit(solution)/shard_map/ppermute | solution.py:20
  17.3 3.7 %collective-permute-start.1 = (bf16[4,69,24,1]{1,2,3,0:T(8,128)(2,1)S(1)}, bf16[4,69,24,1]{1,2,3,0:T(8,128)(2,1)S(1)}, u32[]{:S(2)}, u32[]{:S(2)}) collective-permute-start(bf16[4,69,24,1]{1,2,3,0:T(8,128)(2,1)S(1)} %copy.57), channel_id=1, source_target_pairs={{1,0},{2,1},{3,2},{4,3},{5,4},{6,5},{7,6},{8,7},{9,8},{10,9},{11,1... | collective-permute-start | bytes 39752 | tf_op jit(solution)/shard_map/ppermute | solution.py:23
  22.9 6.8 %copy-start.4 = (bf16[256,256]{1,0:T(8,128)(2,1)S(1)}, bf16[256,256]{1,0:T(8,128)(2,1)}, u32[]{:S(2)}) copy-start(bf16[256,256]{1,0:T(8,128)(2,1)} %param.13) | copy-start | bytes 393220
  24.1 5.7 %collective-permute-start.2 = (bf16[4,69,1,130]{3,1,2,0:T(8,128)(2,1)S(1)}, bf16[4,69,1,130]{3,1,2,0:T(8,128)(2,1)}, u32[]{:S(2)}, u32[]{:S(2)}) collective-permute-start(bf16[4,69,1,130]{3,1,2,0:T(8,128)(2,1)S(1)} %get-tuple-element.150), channel_id=1, source_target_pairs={{0,32},{32,64},{64,96},{1,33},{33,65},{65,97},{2,34},{34,66},{66,9... | collective-permute-start | bytes 215288 | tf_op jit(solution)/shard_map/ppermute | solution.py:20
  28.3 6.0 %collective-permute-start.3 = (bf16[4,69,1,130]{3,1,2,0:T(8,128)(2,1)S(1)}, bf16[4,69,1,130]{3,1,2,0:T(8,128)(2,1)}, u32[]{:S(2)}, u32[]{:S(2)}) collective-permute-start(bf16[4,69,1,130]{3,1,2,0:T(8,128)(2,1)S(1)} %get-tuple-element.151), channel_id=1, source_target_pairs={{32,0},{64,32},{96,64},{33,1},{65,33},{97,65},{34,2},{66,34},{98,6... | collective-permute-start | bytes 215288 | tf_op jit(solution)/shard_map/ppermute | solution.py:23
  29.8 9.7 %copy-start.3 = (bf16[512,128]{1,0:T(8,128)(2,1)S(1)}, bf16[512,128]{1,0:T(8,128)(2,1)}, u32[]{:S(2)}) copy-start(bf16[512,128]{1,0:T(8,128)(2,1)} %param.10) | copy-start | bytes 393220
  39.6 1.3 copy-start.6
  42.9 4.2 %copy-start.1 = (bf16[4,69,26,130]{3,1,2,0:T(8,128)(2,1)S(1)}, bf16[4,69,26,130]{3,1,2,0:T(8,128)(2,1)}, u32[]{:S(2)}) copy-start(bf16[4,69,26,130]{3,1,2,0:T(8,128)(2,1)} %get-tuple-element.281) | copy-start | bytes 5597284 | tf_op jit(solution)/shard_map/while
  42.9 4.2 %copy-start.2 = (bf16[9,128,69]{1,2,0:T(8,128)(2,1)S(1)}, bf16[9,128,69]{1,2,0:T(8,128)(2,1)}, u32[]{:S(2)}) copy-start(bf16[9,128,69]{1,2,0:T(8,128)(2,1)} %get-tuple-element.282) | copy-start | bytes 476932 | tf_op jit(solution)/shard_map/while
  68.9 1.0 copy-start.7
  69.9 1.2 copy-start.6
  73.2 4.2 %copy-start.1 = (bf16[4,69,26,130]{3,1,2,0:T(8,128)(2,1)S(1)}, bf16[4,69,26,130]{3,1,2,0:T(8,128)(2,1)}, u32[]{:S(2)}) copy-start(bf16[4,69,26,130]{3,1,2,0:T(8,128)(2,1)} %get-tuple-element.281) | copy-start | bytes 5597284 | tf_op jit(solution)/shard_map/while
  73.2 4.2 %copy-start.2 = (bf16[9,128,69]{1,2,0:T(8,128)(2,1)S(1)}, bf16[9,128,69]{1,2,0:T(8,128)(2,1)}, u32[]{:S(2)}) copy-start(bf16[9,128,69]{1,2,0:T(8,128)(2,1)} %get-tuple-element.282) | copy-start | bytes 476932 | tf_op jit(solution)/shard_map/while
  99.9 1.0 copy-start.7
  100.8 1.2 copy-start.6
  104.1 4.2 %copy-start.1 = (bf16[4,69,26,130]{3,1,2,0:T(8,128)(2,1)S(1)}, bf16[4,69,26,130]{3,1,2,0:T(8,128)(2,1)}, u32[]{:S(2)}) copy-start(bf16[4,69,26,130]{3,1,2,0:T(8,128)(2,1)} %get-tuple-element.281) | copy-start | bytes 5597284 | tf_op jit(solution)/shard_map/while
  104.1 4.2 %copy-start.2 = (bf16[9,128,69]{1,2,0:T(8,128)(2,1)S(1)}, bf16[9,128,69]{1,2,0:T(8,128)(2,1)}, u32[]{:S(2)}) copy-start(bf16[9,128,69]{1,2,0:T(8,128)(2,1)} %get-tuple-element.282) | copy-start | bytes 476932 | tf_op jit(solution)/shard_map/while
  130.8 1.0 copy-start.7
  270.6 78.1 %copy-start.5 = (f32[256]{0:T(256)S(1)}, f32[256]{0:T(256)}, u32[]{:S(2)}) copy-start(f32[256]{0:T(256)} %param.12) | copy-start | bytes 3076
Sparse Core Ops, SparseCore 0:
  201.9 144.9 all-reduce.1
where the time goes:
time: 358 us; the launch traced here: 357 us
  blocking collectives  132 us (37%)
  waiting for transfers between devices  80.9 us (23%)
  matrix products  61.3 us (17%)
  other arithmetic  33.4 us (9%)
  local copies, waits for them, and re-layouts  24.1 us (7%)
  between operations  14.2 us (4%)
  starting transfers between devices  8.37 us (2%)
    psum x1, waiting for transfers between devices, per_device(): lax.psum((totals * factor, rescale(weighted, factor)), ('lat', 'lon'))  76.4 us
    pmax x1, blocking collectives, per_device(): peak = lax.pmax(maxima, ('lat', 'lon'))  68.2 us
    psum x1, blocking collectives, per_device(): lax.psum((totals * factor, rescale(weighted, factor)), ('lat', 'lon'))  63.9 us
    dot_general x27, matrix products, convolve_block(): jnp.einsum('fc,bcin->bfin', conv_weight[tap_index], piece, preferred_elem...  35.6 us
    convert_element_type x3, other arithmetic, block_terms(): weights_bf = exponent.astype(jnp.bfloat16)  17.2 us
    dot_general x3, matrix products, block_terms(): jnp.einsum('bhqn,bhdn->bqhd', weights_bf, value_heads, preferred_element_...  14.4 us
    dot_general x3, matrix products, block_terms(): jnp.einsum('qhd,bhdn->bhqn', query_heads, key_heads, preferred_element_ty...  7.22 us
  transfers between devices with their start and end apart: 5, of which 2 were waited for; matrix products, arithmetic and copies ran while one was open for 3% of the time, Pallas kernels for 0%

commit v1 on v0

--- a/solution.py
+++ b/solution.py
@@ -1,6 +1,9 @@
+import functools
 import jax
 import jax.numpy as jnp
 from jax import lax
+from jax.experimental import pallas as pl
+from jax.experimental.pallas import tpu as pltpu
 from jax.sharding import PartitionSpec as P
 
 DL = 256
@@ -8,6 +11,148 @@
 HEADS = 4
 HD = 64
 BLK = 8
+MESH = pl.DeviceIdType.MESH
+ROWS = 8
+NCHIP = 64
+
+
+def reduce_kernel(
+    w_ref, st_ref, ow_ref, gain_ref, out_ref,
+    half_w, half_st, msg, recv, own, gath,
+    sem_a, sem_b, sem_c,
+):
+    lat = lax.axis_index("lat")
+    lon = lax.axis_index("lon")
+    core = lax.rem(lon, 2)
+    chip = lat * 16 + lon // 2
+    partner = lon + 1 - 2 * core
+
+    def peer(k):
+        c = lax.rem(chip + k, NCHIP)
+        return (c // 16, lax.rem(c, 16) * 2 + core)
+
+    barrier = pltpu.get_barrier_semaphore()
+    pl.semaphore_signal(barrier, inc=1, device_id=(lat, partner), device_id_type=MESH)
+
+    def greet(k, _):
+        pl.semaphore_signal(barrier, inc=1, device_id=peer(k), device_id_type=MESH)
+        return 0
+
+    lax.fori_loop(1, NCHIP, greet, 0)
+    pl.semaphore_wait(barrier, NCHIP)
+
+    give = 1 - core
+    cw = pltpu.make_async_remote_copy(
+        w_ref.at[give], half_w, sem_a.at[0], sem_a.at[1], device_id=(lat, partner), device_id_type=MESH)
+    cs = pltpu.make_async_remote_copy(
+        st_ref.at[give], half_st, sem_a.at[2], sem_a.at[3], device_id=(lat, partner), device_id_type=MESH)
+    cs.start()
+    cw.start()
+    cs.wait()
+    cw.wait()
+
+    s1 = st_ref[core]
+    s2 = half_st[...]
+    peak = jnp.maximum(s1, s2)
+    f1 = jnp.exp(s1 - peak)
+    f2 = jnp.exp(s2 - peak)
+    lane = lax.broadcasted_iota(jnp.int32, (512, 128), 1)
+    t1 = pltpu.roll(s1, 124, 1)
+    t2 = pltpu.roll(s2, 124, 1)
+    tot = t1 * f1 + t2 * f2
+    for h in range(4):
+        cols = slice(h * 64, h * 64 + 64)
+        val = w_ref[core, :, cols] * f1[:, h:h + 1] + half_w[:, cols] * f2[:, h:h + 1]
+        msg[:, :, cols] = val.reshape(NCHIP, ROWS, 64).astype(jnp.bfloat16)
+
+    def limbs(v):
+        a = v.astype(jnp.bfloat16).astype(jnp.float32)
+        b = (v - a).astype(jnp.bfloat16).astype(jnp.float32)
+        return a, b, v - a - b
+
+    m0, m1, m2 = limbs(jnp.where(lane < 4, peak, 0.0))
+    q0, q1, q2 = limbs(jnp.where(lane < 4, tot, 0.0))
+    packed = (m0 + pltpu.roll(m1, 4, 1) + pltpu.roll(m2, 8, 1)
+              + pltpu.roll(q0, 12, 1) + pltpu.roll(q1, 16, 1) + pltpu.roll(q2, 20, 1))
+    msg[:, :, 256:384] = packed.reshape(NCHIP, ROWS, 128).astype(jnp.bfloat16)
+
+    def scatter(k, _):
+        c = lax.rem(chip + k, NCHIP)
+        pltpu.make_async_remote_copy(
+            msg.at[c], recv.at[k - 1], sem_b.at[0], sem_b.at[1], device_id=peer(k), device_id_type=MESH).start()
+        return 0
+
+    lax.fori_loop(1, NCHIP, scatter, 0)
+    own[...] = msg[chip]
+    pltpu.make_async_copy(recv, recv, sem_b.at[1]).wait()
+
+    def stats(v):
+        m = v + pltpu.roll(v, 124, 1) + pltpu.roll(v, 120, 1)
+        t = pltpu.roll(v, 116, 1) + pltpu.roll(v, 112, 1) + pltpu.roll(v, 108, 1)
+        return m, t
+
+    def unpack(buf):
+        return buf.astype(jnp.float32)
+
+    all_st = jnp.concatenate([recv[:, :, 256:384].astype(jnp.float32), own[:, 256:384].astype(jnp.float32)[None]], axis=0)
+    am, at = stats(all_st.reshape(512, 128))
+    am = am.reshape(NCHIP, ROWS, 128)
+    at = at.reshape(NCHIP, ROWS, 128)
+    top = jnp.max(am, axis=0)
+    fac = jnp.exp(am - top[None])
+    total = jnp.sum(fac * at, axis=0)
+    for h in range(4):
+        cols = slice(h * 64, h * 64 + 64)
+        acc = (jnp.sum(recv[:, :, cols].astype(jnp.float32) * fac[:63, :, h:h + 1], axis=0)
+               + own[:, cols].astype(jnp.float32) * fac[63, :, h:h + 1])
+        gath[core * NCHIP + chip, :, cols] = (acc / total[:, h:h + 1]).astype(jnp.bfloat16)
+    pltpu.make_async_copy(recv, recv, sem_b.at[0]).wait()
+
+    mine = core * NCHIP + chip
+
+    def spread(k, _):
+        pltpu.make_async_remote_copy(
+            gath.at[mine], gath.at[mine], sem_c.at[0], sem_c.at[1], device_id=peer(k), device_id_type=MESH).start()
+        return 0
+
+    lax.fori_loop(1, NCHIP, spread, 0)
+    size = gath.at[pl.ds(0, NCHIP - 1)]
+    pltpu.make_async_copy(size, size, sem_c.at[1]).wait()
+    pltpu.make_async_copy(size, size, sem_c.at[0]).wait()
+    block = gath.at[pl.ds(core * NCHIP, NCHIP)]
+    cg = pltpu.make_async_remote_copy(
+        block, block, sem_c.at[2], sem_c.at[3], device_id=(lat, partner), device_id_type=MESH)
+    cg.start()
+    cg.wait()
+    att = gath[...].astype(jnp.float32).reshape(1024, 256).astype(jnp.bfloat16)
+    proj = jnp.dot(att, ow_ref[...], preferred_element_type=jnp.float32)
+    out_ref[...] = (
+        proj * lax.rsqrt(jnp.mean(proj * proj, axis=-1, keepdims=True) + 1e-06) * gain_ref[...]
+    )
+
+
+def reduce_all(weighted, stats, out_weight, norm_gain):
+    vm = pl.BlockSpec(memory_space=pltpu.VMEM)
+    return pl.pallas_call(
+        reduce_kernel,
+        out_shape=jax.ShapeDtypeStruct((1024, 256), jnp.float32),
+        in_specs=[vm] * 4,
+        out_specs=vm,
+        scratch_shapes=[
+            pltpu.VMEM((512, 256), jnp.float32),
+            pltpu.VMEM((512, 128), jnp.float32),
+            pltpu.VMEM((NCHIP, ROWS, 384), jnp.bfloat16),
+            pltpu.VMEM((NCHIP - 1, ROWS, 384), jnp.bfloat16),
+            pltpu.VMEM((ROWS, 384), jnp.bfloat16),
+            pltpu.VMEM((2 * NCHIP, ROWS, 256), jnp.bfloat16),
+            pltpu.SemaphoreType.DMA((4,)),
+            pltpu.SemaphoreType.DMA((2,)),
+            pltpu.SemaphoreType.DMA((4,)),
+        ],
+        compiler_params=pltpu.CompilerParams(
+            collective_id=1, has_side_effects=True, vmem_limit_bytes=32 * 1024 * 1024
+        ),
+    )(weighted.reshape(2, 512, 256), stats.reshape(2, 512, 128), out_weight, norm_gain.reshape(1, 256))
 
 
 def extended(block, sides, width, periodic):
@@ -110,16 +255,11 @@
         samples, feats.shape[2], lat_rows, lon_cols
     )
     maxima, totals, weighted = running_state
-    peak = lax.pmax(maxima, ("lat", "lon"))
-    factor = jnp.exp(maxima - peak)
-    total_all, weighted_all = lax.psum((totals * factor, rescale(weighted, factor)), ("lat", "lon"))
-    attended = normalize(weighted_all, total_all).astype(jnp.bfloat16)
-    projected = jnp.einsum("bqe,ef->bqf", attended, out_weight, preferred_element_type=jnp.float32)
-    latents = (
-        projected
-        * lax.rsqrt(jnp.mean(projected * projected, axis=-1, keepdims=True) + 1e-06)
-        * norm_gain
-    )
+    stats = jnp.concatenate([maxima, totals], axis=1)
+    stats = jnp.transpose(stats, (0, 2, 1)).reshape(samples * Q, 2 * HEADS)
+    stats = jnp.pad(stats, ((0, 0), (0, 120)))
+    latents = reduce_all(weighted.reshape(samples * Q, DL), stats, out_weight, norm_gain)
+    latents = latents.reshape(samples, Q, DL)
     return (features, latents)
 
 

time: 358 us -> 156 us (0.44)
  blocking collectives: 132 us -> 0 us
  waiting for transfers between devices: 80.9 us -> 4.52 us
  Pallas kernels: 0 us -> 32 us
  between operations: 14.2 us -> 0.8 us
  other arithmetic: 33.4 us -> 22.8 us
    psum x1 -> x0, waiting for transfers between devices: 76.4 us -> none  [per_device(): lax.psum((totals * factor, rescale(weighted, factor)), ('lat', 'lon'))]
    pmax x1 -> x0, blocking collectives: 68.2 us -> none  [per_device(): peak = lax.pmax(maxima, ('lat', 'lon'))]
    psum x1 -> x0, blocking collectives: 63.9 us -> none  [per_device(): lax.psum((totals * factor, rescale(weighted, factor)), ('lat', 'lon'))]
    pallas_call x0 -> x1, Pallas kernels: none -> 32 us  [reduce_all(): pl.pallas_call(reduce_kernel, out_shape=jax.ShapeDtypeStruct((1024, 256),...]
    transpose x6, other arithmetic: 5.61 us -> 0.15 us  [rescale(): jnp.transpose(factor, (0, 2, 1))[..., None]]
  transfers between devices with their start and end apart: 5 -> 4, of which waited for: 2 -> 1; matrix products, arithmetic and copies ran while one was open for 3% -> 3% of each run, Pallas kernels for 0% -> 0%
where the time goes in v1:
time: 156 us; the launch traced here: 155 us
  matrix products  60.9 us (39%)
  Pallas kernels  32 us (21%)
  local copies, waits for them, and re-layouts  22.8 us (15%)
  other arithmetic  22.8 us (15%)
  starting transfers between devices  8.33 us (5%)
  waiting for transfers between devices  4.52 us (3%)
  loops' own time  2.8 us (2%)
    dot_general x27, matrix products, convolve_block(): jnp.einsum('fc,bcin->bfin', conv_weight[tap_index], piece, preferred_elem...  35.6 us
    pallas_call x1, Pallas kernels, reduce_all(): pl.pallas_call(reduce_kernel, out_shape=jax.ShapeDtypeStruct((1024, 256),...  32 us
    convert_element_type x3, other arithmetic, block_terms(): weights_bf = exponent.astype(jnp.bfloat16)  15.3 us
    dot_general x3, matrix products, block_terms(): jnp.einsum('bhqn,bhdn->bqhd', weights_bf, value_heads, preferred_element_...  14.4 us
    dot_general x3, matrix products, block_terms(): jnp.einsum('qhd,bhdn->bhqn', query_heads, key_heads, preferred_element_ty...  7.22 us
    ppermute x2, starting transfers between devices, extended(): lax.ppermute(lax.slice_in_dim(block, block.shape[dim] - width, None, axis...  6.97 us
    unnamed x13, local copies, waits for them, and re-layouts  6.41 us
    concatenate x1, other arithmetic, extended(): block = jnp.concatenate([low, block, high], axis=dim)  5.12 us
  transfers between devices with their start and end apart: 4, of which 1 were waited for; matrix products, arithmetic and copies ran while one was open for 3% of the time, Pallas kernels for 0%

profile of v1, /device:TPU:1, one launch (start us, length us, event | category | flops | bytes accessed | tf_op | source)
XLA Modules:
  0.0 154.9 jit_solution(7543085882205071564)
XLA Ops:
  0.6 4.0 %fusion.70 = (bf16[4,69,24,1]{3,2,1,0:T(8,128)(2,1)}, bf16[4,69,24,1]{3,2,1,0:T(8,128)(2,1)S(1)}) fusion(bf16[4,69,24,128]{3,2,1,0:T(8,128)(2,1)} %param.8), kind=kLoop, calls=%fused_computation.82 | loop fusion | bytes 52992 | tf_op jit(solution)/shard_map/slice | solution.py:166
  4.6 2.2 %copy.48 = bf16[4,69,24,1]{1,2,3,0:T(8,128)(2,1)S(1)} copy(bf16[4,69,24,1]{3,2,1,0:T(8,128)(2,1)} %get-tuple-element.148) | data formatting | bytes 26496
  6.8 2.8 %collective-permute-start = (bf16[4,69,24,1]{1,2,3,0:T(8,128)(2,1)S(1)}, bf16[4,69,24,1]{1,2,3,0:T(8,128)(2,1)S(1)}, u32[]{:S(2)}, u32[]{:S(2)}) collective-permute-start(bf16[4,69,24,1]{1,2,3,0:T(8,128)(2,1)S(1)} %copy.48), channel_id=1, source_target_pairs={{0,1},{1,2},{2,3},{3,4},{4,5},{5,6},{6,7},{7,8},{8,9},{9,10},{10,1... | collective-permute-start | bytes 39752 | tf_op jit(solution)/shard_map/ppermute | solution.py:165
  9.6 1.2 copy.49
  10.8 1.7 %copy.28 = bf16[4,69,24,128]{3,1,2,0:T(8,128)(2,1)S(1)} copy(bf16[4,69,24,128]{3,2,1,0:T(8,128)(2,1)} %param.8) | data formatting | bytes 3391488 | tf_op args[0]
  12.5 1.9 %copy.27 = bf16[4,69,24,1]{3,1,2,0:T(8,128)(2,1)} copy(bf16[4,69,24,1]{1,2,3,0:T(8,128)(2,1)S(1)} %collective-permute-done) | data formatting | bytes 26496 | tf_op jit(solution)/shard_map/ppermute | solution.py:165
  14.5 1.9 %copy.29 = bf16[4,69,24,1]{3,1,2,0:T(8,128)(2,1)} copy(bf16[4,69,24,1]{1,2,3,0:T(8,128)(2,1)S(1)} %collective-permute-done.1) | data formatting | bytes 26496 | tf_op jit(solution)/shard_map/ppermute | solution.py:168
  16.3 1.2 pad_maximum_fusion.3
  17.6 4.2 %collective-permute-start.2 = (bf16[4,69,1,130]{3,1,2,0:T(8,128)(2,1)S(1)}, bf16[4,69,1,130]{3,1,2,0:T(8,128)(2,1)}, u32[]{:S(2)}, u32[]{:S(2)}) collective-permute-start(bf16[4,69,1,130]{3,1,2,0:T(8,128)(2,1)S(1)} %get-tuple-element.146), channel_id=1, source_target_pairs={{0,32},{32,64},{64,96},{1,33},{33,65},{65,97},{2,34},{34,66},{66,9... | collective-permute-start | bytes 215288 | tf_op jit(solution)/shard_map/ppermute | solution.py:165
  21.8 1.3 collective-permute-start.3
  23.2 4.5 %collective-permute-done.3 = bf16[4,69,1,130]{3,1,2,0:T(8,128)(2,1)} collective-permute-done((bf16[4,69,1,130]{3,1,2,0:T(8,128)(2,1)S(1)}, bf16[4,69,1,130]{3,1,2,0:T(8,128)(2,1)}, u32[]{:S(2)}, u32[]{:S(2)}) %collective-permute-start.3) | collective-permute-done | bytes 71792 | tf_op jit(solution)/shard_map/ppermute | solution.py:168
  27.8 5.1 %pad_maximum_fusion = bf16[4,69,26,130]{3,1,2,0:T(8,128)(2,1)} fusion(bf16[4,69,1,130]{3,1,2,0:T(8,128)(2,1)} %collective-permute-done.3, bf16[4,69,24,1]{3,1,2,0:T(8,128)(2,1)} %copy.29, bf16[4,69,24,128]{3,1,2,0:T(8,128)(2,1)S(1)} %copy.28, bf16[4,69,24,1]{3,1,2,0:T(8,128)(2,1)} %copy.27, bf16[4,69,1,130]{3,1,2,0:T(8,128)(2,1)} %collective-permute-done.2), kind=kLoop, calls=%fused_computation.76 | loop fusion | flops 9328800 | bytes 3731520 | tf_op jit(solution)/shard_map/concatenate | solution.py:169
  32.9 83.3 %while.17 = (s32[]{:T(128)}, f32[4,4,256]{2,0,1:T(4,128)S(1)}, f32[4,4,256]{2,0,1:T(4,128)S(1)}, f32[4,256,256]{1,2,0:T(8,128)S(1)}, bf16[3,4,128,8,128]{2,4,3,1...) while((s32[]{:T(128)}, f32[4,4,256]{2,0,1:T(4,128)S(1)}, ...), condition=%wide.region_3.4_spmd.clone, body=%wide.region_0.3_spmd.clone.sunk | while | flops 2299035648 | bytes 122088440 | solution.py:253
  33.1 0.6 dynamic_slice.10
  34.3 2.0 %fusion.129 = f32[4,8,128,128]{3,2,1,0:T(8,128)S(1)} fusion(bf16[4,69,26,130]{3,1,2,0:T(8,128)(2,1)} %get-tuple-element.273, s32[]{:T(128)S(6)} %add.120, s32[]{:T(128)S(6)} %add.122, bf16[9,128,69]{1,2,0:T(8,128)(2,1)S(1)} %get-tuple-element.274), kind=kOutput, calls=%fused_computation.25.clone.1 | convolution fusion | flops 72351744 | bytes 2705416 | tf_op jit(solution)/shard_map/while/body/eval_jaxpr/fc,bcin->bfin/dot_general | solution.py:179
  36.3 2.1 %fusion.131 = f32[4,8,128,128]{3,2,1,0:T(8,128)S(1)} fusion(bf16[4,69,26,130]{3,1,2,0:T(8,128)(2,1)} %get-tuple-element.273, s32[]{:T(128)S(6)} %add.123, s32[]{:T(128)S(6)} %add.121, bf16[9,128,69]{1,2,0:T(8,128)(2,1)S(1)} %get-tuple-element.274), kind=kOutput, calls=%fused_computation.29.clone.1 | convolution fusion | flops 72351744 | bytes 2705416 | tf_op jit(solution)/shard_map/while/body/eval_jaxpr/fc,bcin->bfin/dot_general | solution.py:179
  38.5 2.0 %fusion.132 = f32[4,8,128,128]{3,2,1,0:T(8,128)S(1)} fusion(bf16[4,69,26,130]{3,1,2,0:T(8,128)(2,1)} %get-tuple-element.273, s32[]{:T(128)S(6)} %add.123, s32[]{:T(128)S(6)} %add.122, bf16[9,128,69]{1,2,0:T(8,128)(2,1)S(1)} %get-tuple-element.274), kind=kOutput, calls=%fused_computation.31.clone.1 | convolution fusion | flops 72351744 | bytes 2705416 | tf_op jit(solution)/shard_map/while/body/eval_jaxpr/fc,bcin->bfin/dot_general | solution.py:179
  40.5 0.5 fusion.130
  41.0 0.5 fusion.133
  41.5 0.7 fusion.134
  42.2 0.7 fusion.136
  43.0 0.5 fusion.135
  43.5 2.8 %bitcast_dynamic-update-slice_fusion.2 = (bf16[3,4,128,8,128]{2,4,3,1,0:T(8,128)(2,1)}, bf16[4,128,8,128]{1,3,2,0:T(8,128)(2,1)S(1)}) fusion(bf16[3,4,128,8,128]{2,4,3,1,0:T(8,128)(2,1)} %get-tuple-element.255, s32[]{:T(128)} %get-tuple-element.251, bf16[9,128,69]{1,2,0:T(8,128)(2,1)S(1)} %get-tuple-element.274, ...), kind=kOutput, calls=%fused_computation.21.clone.1 | convolution fusion | flops 81264640 | bytes 19483144 | tf_op jit(solution)/shard_map/while/body/eval_jaxpr/fc,bcin->bfin/dot_general | solution.py:179
  46.3 1.3 convert_bitcast_fusion.2
  47.6 0.4 fusion.137
  48.0 2.4 %bitcast_reduce_fusion.2 = (f32[4,4,256]{2,0,1:T(4,128)S(1)}, f32[4,4,1024,256]{3,2,1,0:T(8,128)S(1)}) fusion(bf16[256,4,64,1]{0,2,3,1:T(8,128)(2,1)S(1)} %bitcast.179, bf16[4,4,64,1024]{3,2,1,0:T(8,128)(2,1)S(1)} %bitcast.176), kind=kOutput, calls=%fused_computation.1.clone.1 | convolution fusion | flops 545255424 | bytes 19021824 | tf_op jit(solution)/shard_map/while/body/eval_jaxpr/qhd,bhdn->bhqn/dot_general | solution.py:196
  50.4 5.1 %fusion.139 = (bf16[4,4,256,1024]{2,3,0,1:T(8,128)(2,1)}, f32[4,4,256]{2,0,1:T(4,128)S(1)}) fusion(f32[4,4,1024,256]{3,2,1,0:T(8,128)S(1)} %get-tuple-element.227, f32[4,4,256]{2,0,1:T(4,128)S(1)} %get-tuple-element.225), kind=kLoop, calls=%fused_computation.3.clone.1 | loop fusion | flops 16773120 | bytes 25198592 | tf_op jit(solution)/shard_map/while/body/eval_jaxpr/convert_element_type | solution.py:202
  55.6 4.8 %fusion.141 = f32[4,256,4,64]{1,3,2,0:T(8,128)S(1)} fusion(bf16[4,4,64,1024]{3,2,1,0:T(8,128)(2,1)S(1)} %bitcast.178, bf16[4,4,256,1024]{2,3,0,1:T(8,128)(2,1)} %get-tuple-element.231, f32[4,256,4]{1,2,0:T(4,128)S(1)} %copy.66), kind=kOutput, calls=%fused_computation.20.clone.1 | convolution fusion | flops 537133056 | bytes 11550720 | tf_op jit(solution)/shard_map/while/body/eval_jaxpr/bhqn,bhdn->bqhd/dot_general | solution.py:203
  60.4 0.3 bitcast_add_fusion.2
  60.8 0.6 dynamic_slice.10
  62.0 2.0 %fusion.129 = f32[4,8,128,128]{3,2,1,0:T(8,128)S(1)} fusion(bf16[4,69,26,130]{3,1,2,0:T(8,128)(2,1)} %get-tuple-element.273, s32[]{:T(128)S(6)} %add.120, s32[]{:T(128)S(6)} %add.122, bf16[9,128,69]{1,2,0:T(8,128)(2,1)S(1)} %get-tuple-element.274), kind=kOutput, calls=%fused_computation.25.clone.1 | convolution fusion | flops 72351744 | bytes 2705416 | tf_op jit(solution)/shard_map/while/body/eval_jaxpr/fc,bcin->bfin/dot_general | solution.py:179
  64.0 2.1 %fusion.131 = f32[4,8,128,128]{3,2,1,0:T(8,128)S(1)} fusion(bf16[4,69,26,130]{3,1,2,0:T(8,128)(2,1)} %get-tuple-element.273, s32[]{:T(128)S(6)} %add.123, s32[]{:T(128)S(6)} %add.121, bf16[9,128,69]{1,2,0:T(8,128)(2,1)S(1)} %get-tuple-element.274), kind=kOutput, calls=%fused_computation.29.clone.1 | convolution fusion | flops 72351744 | bytes 2705416 | tf_op jit(solution)/shard_map/while/body/eval_jaxpr/fc,bcin->bfin/dot_general | solution.py:179
  66.2 2.0 %fusion.132 = f32[4,8,128,128]{3,2,1,0:T(8,128)S(1)} fusion(bf16[4,69,26,130]{3,1,2,0:T(8,128)(2,1)} %get-tuple-element.273, s32[]{:T(128)S(6)} %add.123, s32[]{:T(128)S(6)} %add.122, bf16[9,128,69]{1,2,0:T(8,128)(2,1)S(1)} %get-tuple-element.274), kind=kOutput, calls=%fused_computation.31.clone.1 | convolution fusion | flops 72351744 | bytes 2705416 | tf_op jit(solution)/shard_map/while/body/eval_jaxpr/fc,bcin->bfin/dot_general | solution.py:179
  68.2 0.5 fusion.130
  68.7 0.5 fusion.133
  69.2 0.7 fusion.134
  69.9 0.7 fusion.136
  70.6 0.5 fusion.135
  71.2 2.8 %bitcast_dynamic-update-slice_fusion.2 = (bf16[3,4,128,8,128]{2,4,3,1,0:T(8,128)(2,1)}, bf16[4,128,8,128]{1,3,2,0:T(8,128)(2,1)S(1)}) fusion(bf16[3,4,128,8,128]{2,4,3,1,0:T(8,128)(2,1)} %get-tuple-element.255, s32[]{:T(128)} %get-tuple-element.251, bf16[9,128,69]{1,2,0:T(8,128)(2,1)S(1)} %get-tuple-element.274, ...), kind=kOutput, calls=%fused_computation.21.clone.1 | convolution fusion | flops 81264640 | bytes 19483144 | tf_op jit(solution)/shard_map/while/body/eval_jaxpr/fc,bcin->bfin/dot_general | solution.py:179
  73.9 1.3 convert_bitcast_fusion.2
  75.2 0.4 fusion.137
  75.6 2.4 %bitcast_reduce_fusion.2 = (f32[4,4,256]{2,0,1:T(4,128)S(1)}, f32[4,4,1024,256]{3,2,1,0:T(8,128)S(1)}) fusion(bf16[256,4,64,1]{0,2,3,1:T(8,128)(2,1)S(1)} %bitcast.179, bf16[4,4,64,1024]{3,2,1,0:T(8,128)(2,1)S(1)} %bitcast.176), kind=kOutput, calls=%fused_computation.1.clone.1 | convolution fusion | flops 545255424 | bytes 19021824 | tf_op jit(solution)/shard_map/while/body/eval_jaxpr/qhd,bhdn->bhqn/dot_general | solution.py:196
  78.0 5.1 %fusion.139 = (bf16[4,4,256,1024]{2,3,0,1:T(8,128)(2,1)}, f32[4,4,256]{2,0,1:T(4,128)S(1)}) fusion(f32[4,4,1024,256]{3,2,1,0:T(8,128)S(1)} %get-tuple-element.227, f32[4,4,256]{2,0,1:T(4,128)S(1)} %get-tuple-element.225), kind=kLoop, calls=%fused_computation.3.clone.1 | loop fusion | flops 16773120 | bytes 25198592 | tf_op jit(solution)/shard_map/while/body/eval_jaxpr/convert_element_type | solution.py:202
  83.2 4.8 %fusion.141 = f32[4,256,4,64]{1,3,2,0:T(8,128)S(1)} fusion(bf16[4,4,64,1024]{3,2,1,0:T(8,128)(2,1)S(1)} %bitcast.178, bf16[4,4,256,1024]{2,3,0,1:T(8,128)(2,1)} %get-tuple-element.231, f32[4,256,4]{1,2,0:T(4,128)S(1)} %copy.66), kind=kOutput, calls=%fused_computation.20.clone.1 | convolution fusion | flops 537133056 | bytes 11550720 | tf_op jit(solution)/shard_map/while/body/eval_jaxpr/bhqn,bhdn->bqhd/dot_general | solution.py:203
  88.0 0.3 bitcast_add_fusion.2
  88.4 0.6 dynamic_slice.10
  89.6 2.0 %fusion.129 = f32[4,8,128,128]{3,2,1,0:T(8,128)S(1)} fusion(bf16[4,69,26,130]{3,1,2,0:T(8,128)(2,1)} %get-tuple-element.273, s32[]{:T(128)S(6)} %add.120, s32[]{:T(128)S(6)} %add.122, bf16[9,128,69]{1,2,0:T(8,128)(2,1)S(1)} %get-tuple-element.274), kind=kOutput, calls=%fused_computation.25.clone.1 | convolution fusion | flops 72351744 | bytes 2705416 | tf_op jit(solution)/shard_map/while/body/eval_jaxpr/fc,bcin->bfin/dot_general | solution.py:179
  91.6 2.1 %fusion.131 = f32[4,8,128,128]{3,2,1,0:T(8,128)S(1)} fusion(bf16[4,69,26,130]{3,1,2,0:T(8,128)(2,1)} %get-tuple-element.273, s32[]{:T(128)S(6)} %add.123, s32[]{:T(128)S(6)} %add.121, bf16[9,128,69]{1,2,0:T(8,128)(2,1)S(1)} %get-tuple-element.274), kind=kOutput, calls=%fused_computation.29.clone.1 | convolution fusion | flops 72351744 | bytes 2705416 | tf_op jit(solution)/shard_map/while/body/eval_jaxpr/fc,bcin->bfin/dot_general | solution.py:179
  93.8 2.0 %fusion.132 = f32[4,8,128,128]{3,2,1,0:T(8,128)S(1)} fusion(bf16[4,69,26,130]{3,1,2,0:T(8,128)(2,1)} %get-tuple-element.273, s32[]{:T(128)S(6)} %add.123, s32[]{:T(128)S(6)} %add.122, bf16[9,128,69]{1,2,0:T(8,128)(2,1)S(1)} %get-tuple-element.274), kind=kOutput, calls=%fused_computation.31.clone.1 | convolution fusion | flops 72351744 | bytes 2705416 | tf_op jit(solution)/shard_map/while/body/eval_jaxpr/fc,bcin->bfin/dot_general | solution.py:179
  95.8 0.5 fusion.130
  96.3 0.5 fusion.133
  96.8 0.7 fusion.134
  97.5 0.7 fusion.136
  98.3 0.5 fusion.135
  98.8 2.7 %bitcast_dynamic-update-slice_fusion.2 = (bf16[3,4,128,8,128]{2,4,3,1,0:T(8,128)(2,1)}, bf16[4,128,8,128]{1,3,2,0:T(8,128)(2,1)S(1)}) fusion(bf16[3,4,128,8,128]{2,4,3,1,0:T(8,128)(2,1)} %get-tuple-element.255, s32[]{:T(128)} %get-tuple-element.251, bf16[9,128,69]{1,2,0:T(8,128)(2,1)S(1)} %get-tuple-element.274, ...), kind=kOutput, calls=%fused_computation.21.clone.1 | convolution fusion | flops 81264640 | bytes 19483144 | tf_op jit(solution)/shard_map/while/body/eval_jaxpr/fc,bcin->bfin/dot_general | solution.py:179
  101.5 1.3 convert_bitcast_fusion.2
  102.8 0.4 fusion.137
  103.2 2.4 %bitcast_reduce_fusion.2 = (f32[4,4,256]{2,0,1:T(4,128)S(1)}, f32[4,4,1024,256]{3,2,1,0:T(8,128)S(1)}) fusion(bf16[256,4,64,1]{0,2,3,1:T(8,128)(2,1)S(1)} %bitcast.179, bf16[4,4,64,1024]{3,2,1,0:T(8,128)(2,1)S(1)} %bitcast.176), kind=kOutput, calls=%fused_computation.1.clone.1 | convolution fusion | flops 545255424 | bytes 19021824 | tf_op jit(solution)/shard_map/while/body/eval_jaxpr/qhd,bhdn->bhqn/dot_general | solution.py:196
  105.7 5.1 %fusion.139 = (bf16[4,4,256,1024]{2,3,0,1:T(8,128)(2,1)}, f32[4,4,256]{2,0,1:T(4,128)S(1)}) fusion(f32[4,4,1024,256]{3,2,1,0:T(8,128)S(1)} %get-tuple-element.227, f32[4,4,256]{2,0,1:T(4,128)S(1)} %get-tuple-element.225), kind=kLoop, calls=%fused_computation.3.clone.1 | loop fusion | flops 16773120 | bytes 25198592 | tf_op jit(solution)/shard_map/while/body/eval_jaxpr/convert_element_type | solution.py:202
  110.8 4.8 %fusion.141 = f32[4,256,4,64]{1,3,2,0:T(8,128)S(1)} fusion(bf16[4,4,64,1024]{3,2,1,0:T(8,128)(2,1)S(1)} %bitcast.178, bf16[4,4,256,1024]{2,3,0,1:T(8,128)(2,1)} %get-tuple-element.231, f32[4,256,4]{1,2,0:T(4,128)S(1)} %copy.66), kind=kOutput, calls=%fused_computation.20.clone.1 | convolution fusion | flops 537133056 | bytes 11550720 | tf_op jit(solution)/shard_map/while/body/eval_jaxpr/bhqn,bhdn->bqhd/dot_general | solution.py:203
  116.5 0.3 copy.32
  117.1 32.0 %shard_map.77 = f32[1024,256]{1,0:T(8,128)S(1)} custom-call(f32[2,512,256]{2,1,0:T(8,128)S(1)} %bitcast.173, f32[2,512,128]{2,1,0:T(8,128)S(1)} %bitcast.174, bf16[256,256]{1,0:T(8,128)(2,1)S(1)} %copy-done, f32[1,256]{1,0:T(1,128)S(1)} %bitcast.175), custom_call_target="tpu_custom_call" | custom-call | tf_op jit(solution)/shard_map/pallas_call | solution.py:136
  149.1 4.8 %copy.31 = bf16[4,128,3,8,128]{4,3,2,1,0:T(8,128)(2,1)} copy(bf16[4,128,3,8,128]{1,4,3,0,2:T(8,128)(2,1)} %bitcast.180) | data formatting | bytes 6291456 | tf_op jit(solution)/shard_map/transpose | solution.py:254
  153.9 1.0 copy.85
  (49 shorter events, 1.3 us)
Async XLA Ops:
  6.8 5.7 %collective-permute-start = (bf16[4,69,24,1]{1,2,3,0:T(8,128)(2,1)S(1)}, bf16[4,69,24,1]{1,2,3,0:T(8,128)(2,1)S(1)}, u32[]{:S(2)}, u32[]{:S(2)}) collective-permute-start(bf16[4,69,24,1]{1,2,3,0:T(8,128)(2,1)S(1)} %copy.48), channel_id=1, source_target_pairs={{0,1},{1,2},{2,3},{3,4},{4,5},{5,6},{6,7},{7,8},{8,9},{9,10},{10,1... | collective-permute-start | bytes 39752 | tf_op jit(solution)/shard_map/ppermute | solution.py:165
  10.8 3.7 %collective-permute-start.1 = (bf16[4,69,24,1]{1,2,3,0:T(8,128)(2,1)S(1)}, bf16[4,69,24,1]{1,2,3,0:T(8,128)(2,1)S(1)}, u32[]{:S(2)}, u32[]{:S(2)}) collective-permute-start(bf16[4,69,24,1]{1,2,3,0:T(8,128)(2,1)S(1)} %copy.49), channel_id=1, source_target_pairs={{1,0},{2,1},{3,2},{4,3},{5,4},{6,5},{7,6},{8,7},{9,8},{10,9},{11,1... | collective-permute-start | bytes 39752 | tf_op jit(solution)/shard_map/ppermute | solution.py:168
  16.3 6.8 %copy-start.5 = (bf16[256,256]{1,0:T(8,128)(2,1)S(1)}, bf16[256,256]{1,0:T(8,128)(2,1)}, u32[]{:S(2)}) copy-start(bf16[256,256]{1,0:T(8,128)(2,1)} %param.13) | copy-start | bytes 393220
  17.6 5.7 %collective-permute-start.2 = (bf16[4,69,1,130]{3,1,2,0:T(8,128)(2,1)S(1)}, bf16[4,69,1,130]{3,1,2,0:T(8,128)(2,1)}, u32[]{:S(2)}, u32[]{:S(2)}) collective-permute-start(bf16[4,69,1,130]{3,1,2,0:T(8,128)(2,1)S(1)} %get-tuple-element.146), channel_id=1, source_target_pairs={{0,32},{32,64},{64,96},{1,33},{33,65},{65,97},{2,34},{34,66},{66,9... | collective-permute-start | bytes 215288 | tf_op jit(solution)/shard_map/ppermute | solution.py:165
  21.8 6.0 %collective-permute-start.3 = (bf16[4,69,1,130]{3,1,2,0:T(8,128)(2,1)S(1)}, bf16[4,69,1,130]{3,1,2,0:T(8,128)(2,1)}, u32[]{:S(2)}, u32[]{:S(2)}) collective-permute-start(bf16[4,69,1,130]{3,1,2,0:T(8,128)(2,1)S(1)} %get-tuple-element.147), channel_id=1, source_target_pairs={{32,0},{64,32},{96,64},{33,1},{65,33},{97,65},{34,2},{66,34},{98,6... | collective-permute-start | bytes 215288 | tf_op jit(solution)/shard_map/ppermute | solution.py:168
  23.2 9.7 %copy-start.3 = (bf16[9,128,69]{1,2,0:T(8,128)(2,1)S(1)}, bf16[9,128,69]{1,2,0:T(8,128)(2,1)}, u32[]{:S(2)}) copy-start(bf16[9,128,69]{1,2,0:T(8,128)(2,1)} %param.9) | copy-start | bytes 476932
  36.3 4.2 %copy-start.2 = (bf16[4,69,26,130]{3,1,2,0:T(8,128)(2,1)S(1)}, bf16[4,69,26,130]{3,1,2,0:T(8,128)(2,1)}, u32[]{:S(2)}) copy-start(bf16[4,69,26,130]{3,1,2,0:T(8,128)(2,1)} %get-tuple-element.273) | copy-start | bytes 5597284 | tf_op jit(solution)/shard_map/while
  43.5 2.8 %copy-start.4 = (bf16[512,128]{1,0:T(8,128)(2,1)S(1)}, bf16[512,128]{1,0:T(8,128)(2,1)}, u32[]{:S(2)}) copy-start(bf16[512,128]{1,0:T(8,128)(2,1)} %get-tuple-element.275) | copy-start | bytes 393220 | tf_op jit(solution)/shard_map/while
  64.0 4.2 %copy-start.2 = (bf16[4,69,26,130]{3,1,2,0:T(8,128)(2,1)S(1)}, bf16[4,69,26,130]{3,1,2,0:T(8,128)(2,1)}, u32[]{:S(2)}) copy-start(bf16[4,69,26,130]{3,1,2,0:T(8,128)(2,1)} %get-tuple-element.273) | copy-start | bytes 5597284 | tf_op jit(solution)/shard_map/while
  71.2 2.8 %copy-start.4 = (bf16[512,128]{1,0:T(8,128)(2,1)S(1)}, bf16[512,128]{1,0:T(8,128)(2,1)}, u32[]{:S(2)}) copy-start(bf16[512,128]{1,0:T(8,128)(2,1)} %get-tuple-element.275) | copy-start | bytes 393220 | tf_op jit(solution)/shard_map/while
  91.6 4.2 %copy-start.2 = (bf16[4,69,26,130]{3,1,2,0:T(8,128)(2,1)S(1)}, bf16[4,69,26,130]{3,1,2,0:T(8,128)(2,1)}, u32[]{:S(2)}) copy-start(bf16[4,69,26,130]{3,1,2,0:T(8,128)(2,1)} %get-tuple-element.273) | copy-start | bytes 5597284 | tf_op jit(solution)/shard_map/while
  98.8 2.8 %copy-start.4 = (bf16[512,128]{1,0:T(8,128)(2,1)S(1)}, bf16[512,128]{1,0:T(8,128)(2,1)}, u32[]{:S(2)}) copy-start(bf16[512,128]{1,0:T(8,128)(2,1)} %get-tuple-element.275) | copy-start | bytes 393220 | tf_op jit(solution)/shard_map/while
  116.2 0.9 copy-start
  116.2 0.9 copy-start.1

commit v2 on v1

--- a/solution.py
+++ b/solution.py
@@ -10,7 +10,6 @@
 Q = 256
 HEADS = 4
 HD = 64
-BLK = 8
 MESH = pl.DeviceIdType.MESH
 ROWS = 8
 NCHIP = 64
@@ -155,112 +154,277 @@
     )(weighted.reshape(2, 512, 256), stats.reshape(2, 512, 128), out_weight, norm_gain.reshape(1, 256))
 
 
-def extended(block, sides, width, periodic):
-    for axis, dim in sides:
-        count = lax.axis_size(axis)
-        forward = [(i, i + 1) for i in range(count - 1)]
-        if periodic:
-            forward.append((count - 1, 0))
-        backward = [(target, source) for source, target in forward]
-        low = lax.ppermute(
-            lax.slice_in_dim(block, block.shape[dim] - width, None, axis=dim), axis, forward
-        )
-        high = lax.ppermute(lax.slice_in_dim(block, 0, width, axis=dim), axis, backward)
-        block = jnp.concatenate([low, block, high], axis=dim)
-    return block
-
-
-def convolve_block(window_in, conv_weight, lat_rows, lon_cols):
-    running = jnp.zeros((window_in.shape[0], conv_weight.shape[1], lat_rows, lon_cols), jnp.float32)
-    for tap_index in range(9):
-        row_off = tap_index // 3
-        col_off = tap_index % 3
-        piece = window_in[:, :, row_off : row_off + lat_rows, col_off : col_off + lon_cols]
-        running = running + jnp.einsum(
-            "fc,bcin->bfin", conv_weight[tap_index], piece, preferred_element_type=jnp.float32
-        )
-    return running
-
-
-def block_terms(window_in, conv_weight, kv_weight, queries, lat_rows, lon_cols):
-    samples = window_in.shape[0]
-    convolved = convolve_block(window_in, conv_weight, lat_rows, lon_cols)
-    block_features = jax.nn.gelu(convolved, approximate=True).astype(jnp.bfloat16)
-    flattened = block_features.reshape(samples, block_features.shape[1], lat_rows * lon_cols)
-    key_value = jnp.einsum(
-        "of,bfn->bon", kv_weight, flattened, preferred_element_type=jnp.float32
-    ).astype(jnp.bfloat16)
-    key_heads = key_value[:, :DL].reshape(samples, HEADS, HD, lat_rows * lon_cols)
-    value_heads = key_value[:, DL:].reshape(samples, HEADS, HD, lat_rows * lon_cols)
-    query_heads = queries.reshape(Q, HEADS, HD)
-    scores = jnp.einsum(
-        "qhd,bhdn->bhqn", query_heads, key_heads, preferred_element_type=jnp.float32
-    ) * HD ** (-0.5)
-    maxima = jnp.max(scores, axis=-1)
-    exponent = jnp.exp(scores - maxima[..., None])
-    totals = jnp.sum(exponent, axis=-1)
-    weights_bf = exponent.astype(jnp.bfloat16)
-    weighted = jnp.einsum(
-        "bhqn,bhdn->bqhd", weights_bf, value_heads, preferred_element_type=jnp.float32
-    )
-    return (block_features, maxima, totals, weighted.reshape(samples, Q, DL))
-
-
-def rescale(weighted, factor):
-    full_shape = weighted.shape
-    heads_view = weighted.reshape(full_shape[0], full_shape[1], factor.shape[1], -1)
-    return (heads_view * jnp.transpose(factor, (0, 2, 1))[..., None]).reshape(full_shape)
-
-
-def normalize(weighted, totals):
-    full_shape = weighted.shape
-    heads_view = weighted.reshape(full_shape[0], full_shape[1], totals.shape[1], -1)
-    return (heads_view / jnp.transpose(totals, (0, 2, 1))[..., None]).reshape(full_shape)
-
-
-def combine_partial(earlier, later):
-    highest = jnp.maximum(earlier[0], later[0])
-    scale_one = jnp.exp(earlier[0] - highest)
-    scale_two = jnp.exp(later[0] - highest)
-    totals = earlier[1] * scale_one + later[1] * scale_two
-    weighted = rescale(earlier[2], scale_one) + rescale(later[2], scale_two)
-    return (highest, totals, weighted)
+CP = 80
+KROW = 3 * CP
+SCALE = HD ** (-0.5)
+NT = (((1,), (1,)), ((), ()))
+
+
+def halo_kernel(
+    xt_ref, cw_ref, kv_ref, rows_ref, cols_ref, w2_ref, kv2_ref,
+    edge, got, taps, send_sem, recv_sem,
+):
+    lat = lax.axis_index("lat")
+    lon = lax.axis_index("lon")
+    nlat = lax.axis_size("lat")
+    nlon = lax.axis_size("lon")
+    right = lax.rem(lon + 1, nlon)
+    left = lax.rem(lon + nlon - 1, nlon)
+    barrier = pltpu.get_barrier_semaphore()
+
+    def greet(dlat, dlon):
+        pl.semaphore_signal(barrier, inc=1, device_id=(dlat, dlon), device_id_type=MESH)
+
+    greet(lat, left)
+    greet(lat, right)
+
+    @pl.when(lat > 0)
+    def _():
+        greet(lat - 1, left)
+        greet(lat - 1, lon)
+        greet(lat - 1, right)
+
+    @pl.when(lat < nlat - 1)
+    def _():
+        greet(lat + 1, left)
+        greet(lat + 1, lon)
+        greet(lat + 1, right)
+
+    lane = lax.broadcasted_iota(jnp.int32, (CP, 128), 1)
+    last = jnp.zeros((CP, 128), jnp.float32)
+    first = jnp.zeros((CP, 128), jnp.float32)
+    for b in range(xt_ref.shape[0]):
+        for i in range(24):
+            at = b * 24 + i
+            row = xt_ref[b, i].astype(jnp.float32)
+            last = jnp.where(lane == at, pltpu.roll(row, (at + 1) % 128, 1), last)
+            first = jnp.where(lane == at, pltpu.roll(row, at, 1), first)
+    edge[0] = last.astype(jnp.bfloat16)
+    edge[1] = first.astype(jnp.bfloat16)
+
+    def copy(src, dst, n, dlat, dlon):
+        return pltpu.make_async_remote_copy(
+            src, dst, send_sem.at[n], recv_sem.at[n], device_id=(dlat, dlon), device_id_type=MESH)
+
+    same = [
+        copy(edge.at[0], got.at[0, 0], 0, lat, right),
+        copy(edge.at[1], got.at[1, 0], 1, lat, left),
+    ]
+    down = [
+        copy(xt_ref.at[:, 23], rows_ref.at[0], 2, lat + 1, lon),
+        copy(edge.at[0], got.at[0, 1], 3, lat + 1, right),
+        copy(edge.at[1], got.at[1, 1], 4, lat + 1, left),
+    ]
+    up = [
+        copy(xt_ref.at[:, 0], rows_ref.at[1], 5, lat - 1, lon),
+        copy(edge.at[0], got.at[0, 2], 6, lat - 1, right),
+        copy(edge.at[1], got.at[1, 2], 7, lat - 1, left),
+    ]
+    inner = jnp.logical_and(lat > 0, lat < nlat - 1)
+
+    @pl.when(inner)
+    def _():
+        pl.semaphore_wait(barrier, 8)
+
+    @pl.when(jnp.logical_not(inner))
+    def _():
+        pl.semaphore_wait(barrier, 5)
+
+    for c in same:
+        c.start()
+
+    @pl.when(lat < nlat - 1)
+    def _():
+        for c in down:
+            c.start()
+
+    @pl.when(lat > 0)
+    def _():
+        for c in up:
+            c.start()
+
+    taps[...] = jnp.zeros_like(taps)
+    for t in range(9):
+        value = cw_ref[t].astype(jnp.float32)
+        value = jnp.concatenate([value, jnp.zeros((CP - value.shape[0], 128), jnp.float32)], axis=0).astype(jnp.bfloat16)
+        taps[t * CP:(t + 1) * CP, 0:128] = value
+        taps[KROW + t * CP:KROW + (t + 1) * CP, 128:256] = value
+    out_at = lax.broadcasted_iota(jnp.int32, (256, 256), 0)
+    in_at = lax.broadcasted_iota(jnp.int32, (256, 256), 1)
+    spread = jnp.where(out_at == jnp.where(in_at < 128, 2 * in_at, 2 * in_at - 255), 1.0, 0.0).astype(jnp.bfloat16)
+    w2_ref[...] = lax.dot_general(spread, taps[...], NT, preferred_element_type=jnp.float32).astype(jnp.bfloat16)
+    for r in range(2):
+        kv2_ref[r * 512:(r + 1) * 512] = lax.dot_general(
+            kv_ref[...], spread[:, r * 128:(r + 1) * 128], NT, preferred_element_type=jnp.float32).astype(jnp.bfloat16)
+
+    for c in same:
+        c.wait()
+
+    @pl.when(lat > 0)
+    def _():
+        for c in down:
+            c.wait_recv()
+        for c in up:
+            c.wait_send()
+
+    @pl.when(lat < nlat - 1)
+    def _():
+        for c in up:
+            c.wait_recv()
+        for c in down:
+            c.wait_send()
+
+    @pl.when(lat == 0)
+    def _():
+        rows_ref[0] = jnp.zeros_like(rows_ref[0])
+        for side in range(2):
+            got[side, 1] = jnp.zeros((CP, 128), jnp.bfloat16)
+
+    @pl.when(lat == nlat - 1)
+    def _():
+        rows_ref[1] = jnp.zeros_like(rows_ref[1])
+        for side in range(2):
+            got[side, 2] = jnp.zeros((CP, 128), jnp.bfloat16)
+
+    for side in range(2):
+        mid = got[side, 0].astype(jnp.float32)
+        above = got[side, 1].astype(jnp.float32)
+        below = got[side, 2].astype(jnp.float32)
+        for b in range(4):
+            value = pltpu.roll(mid, (129 - b * 24) % 128, 1)
+            value = jnp.where(lane == 0, pltpu.roll(above, (128 - b * 24 - 23) % 128, 1), value)
+            value = jnp.where(lane == 25, pltpu.roll(below, (128 + 25 - b * 24) % 128, 1), value)
+            cols_ref[side, b] = value.astype(jnp.bfloat16)
+
+
+def halo(xt, conv_t, kv_weight):
+    vm = pl.BlockSpec(memory_space=pltpu.VMEM)
+    samples = xt.shape[0]
+    return pl.pallas_call(
+        halo_kernel,
+        out_shape=(
+            jax.ShapeDtypeStruct((2, samples, CP, 128), jnp.bfloat16),
+            jax.ShapeDtypeStruct((2, samples, CP, 128), jnp.bfloat16),
+            jax.ShapeDtypeStruct((256, 4 * KROW), jnp.bfloat16),
+            jax.ShapeDtypeStruct((1024, 256), jnp.bfloat16),
+        ),
+        in_specs=[vm] * 3,
+        out_specs=(vm,) * 4,
+        scratch_shapes=[
+            pltpu.VMEM((2, CP, 128), jnp.bfloat16),
+            pltpu.VMEM((2, 3, CP, 128), jnp.bfloat16),
+            pltpu.VMEM((4 * KROW, 256), jnp.bfloat16),
+            pltpu.SemaphoreType.DMA((8,)),
+            pltpu.SemaphoreType.DMA((8,)),
+        ],
+        compiler_params=pltpu.CompilerParams(
+            collective_id=0, has_side_effects=True, vmem_limit_bytes=32 * 1024 * 1024),
+    )(xt, conv_t, kv_weight)
+
+
+def encode_kernel(
+    xt_ref, rows_ref, cols_ref, w2_ref, kv2_ref, q_ref, feat_ref, w_out, st_out,
+    x3, qs, kvs, run,
+):
+    chunk = pl.program_id(1)
+    lane = lax.broadcasted_iota(jnp.int32, (CP, 128), 1)
+
+    @pl.when(chunk == 0)
+    def _():
+        for h in range(HEADS):
+            qs[h] = (q_ref[:, h * HD:(h + 1) * HD].astype(jnp.float32) * SCALE).astype(jnp.bfloat16)
+        lo = cols_ref[0, 0].astype(jnp.float32)
+        hi = cols_ref[1, 0].astype(jnp.float32)
+        for i in range(26):
+            row = rows_ref[0, 0] if i == 0 else rows_ref[1, 0] if i == 25 else xt_ref[0, i - 1]
+            wide = row.astype(jnp.float32)
+            before = jnp.where(lane == 0, pltpu.roll(lo, (128 - i) % 128, 1), pltpu.roll(wide, 1, 1))
+            after = jnp.where(lane == 127, pltpu.roll(hi, 127 - i, 1), pltpu.roll(wide, 127, 1))
+            x3[i, 0:CP] = before.astype(jnp.bfloat16)
+            x3[i, CP:2 * CP] = row
+            x3[i, 2 * CP:3 * CP] = after.astype(jnp.bfloat16)
+
+    w2 = w2_ref[...]
+    for g in range(2):
+        base = chunk * 8 + g * 4
+        one = x3[pl.ds(base, 4)].reshape(4 * KROW, 128)
+        two = x3[pl.ds(base + 2, 4)].reshape(4 * KROW, 128)
+        both = jnp.concatenate([one, two], axis=1)
+        conv = jnp.dot(w2, both, preferred_element_type=jnp.float32)
+        feats = jax.nn.gelu(conv, approximate=True).astype(jnp.bfloat16)
+        feat_ref[0, :, 2 * g] = feats[:, 0:128].reshape(128, 2, 128)
+        feat_ref[0, :, 2 * g + 1] = feats[:, 128:256].reshape(128, 2, 128)
+        kvs[:, g * 256:(g + 1) * 256] = jnp.dot(
+            kv2_ref[...], feats, preferred_element_type=jnp.float32).astype(jnp.bfloat16)
+
+    st_lane = lax.broadcasted_iota(jnp.int32, (256, 128), 1)
+    old = jnp.where(chunk == 0, jnp.where(st_lane < 4, -3e38, 0.0), run[...])
+    new = jnp.zeros((256, 128), jnp.float32)
+    for h in range(HEADS):
+        rows = slice(h * HD, (h + 1) * HD)
+        s0 = jnp.dot(qs[h], kvs[rows], preferred_element_type=jnp.float32)
+        s1 = jnp.dot(qs[h], kvs[512 + h * HD:512 + (h + 1) * HD], preferred_element_type=jnp.float32)
+        top = jnp.max(jnp.maximum(s0, s1), axis=1, keepdims=True)
+        before = old[:, h:h + 1]
+        peak = jnp.maximum(before, top)
+        mine = jnp.exp(top - peak)
+        keep = jnp.exp(before - peak)
+        p0 = jnp.exp(s0 - top)
+        p1 = jnp.exp(s1 - top)
+        total = jnp.sum(p0 + p1, axis=1, keepdims=True)
+        v0 = kvs[256 + h * HD:256 + (h + 1) * HD]
+        v1 = kvs[768 + h * HD:768 + (h + 1) * HD]
+        part = (lax.dot_general(p0.astype(jnp.bfloat16), v0, NT, preferred_element_type=jnp.float32)
+                + lax.dot_general(p1.astype(jnp.bfloat16), v1, NT, preferred_element_type=jnp.float32))
+        sofar = jnp.where(chunk == 0, 0.0, w_out[0, :, rows])
+        w_out[0, :, rows] = sofar * keep + part * mine
+        total = old[:, 4 + h:5 + h] * keep + total * mine
+        new = jnp.where(st_lane == h, peak, jnp.where(st_lane == 4 + h, total, new))
+    run[...] = new
+    st_out[0] = new
+
+
+def encode(xt, rows, cols, w2, kv2, queries):
+    samples = xt.shape[0]
+    whole = pl.BlockSpec(memory_space=pltpu.VMEM)
+    side = pl.BlockSpec((2, 1, CP, 128), lambda b, c: (0, b, 0, 0))
+    return pl.pallas_call(
+        encode_kernel,
+        grid=(samples, 3),
+        out_shape=(
+            jax.ShapeDtypeStruct((samples, 128, 12, 2, 128), jnp.bfloat16),
+            jax.ShapeDtypeStruct((samples, Q, DL), jnp.float32),
+            jax.ShapeDtypeStruct((samples, Q, 128), jnp.float32),
+        ),
+        in_specs=[
+            pl.BlockSpec((1, 24, CP, 128), lambda b, c: (b, 0, 0, 0)),
+            side, side, whole, whole, whole,
+        ],
+        out_specs=(
+            pl.BlockSpec((1, 128, 4, 2, 128), lambda b, c: (b, 0, c, 0, 0)),
+            pl.BlockSpec((1, Q, DL), lambda b, c: (b, 0, 0)),
+            pl.BlockSpec((1, Q, 128), lambda b, c: (b, 0, 0)),
+        ),
+        scratch_shapes=[
+            pltpu.VMEM((26, KROW, 128), jnp.bfloat16),
+            pltpu.VMEM((HEADS, Q, HD), jnp.bfloat16),
+            pltpu.VMEM((1024, 512), jnp.bfloat16),
+            pltpu.VMEM((Q, 128), jnp.float32),
+        ],
+        compiler_params=pltpu.CompilerParams(
+            dimension_semantics=("arbitrary", "arbitrary"), vmem_limit_bytes=48 * 1024 * 1024),
+    )(xt, rows, cols, w2, kv2, queries)
 
 
 def per_device(fields, conv_weight, kv_weight, out_weight, norm_gain, queries):
     samples, channels, lat_rows, lon_cols = fields.shape
-    widened = extended(fields, (("lon", 3),), 1, True)
-    padded = extended(widened, (("lat", 2),), 1, False)
-    block_count = lat_rows // BLK
-    initial = (
-        jnp.full((samples, HEADS, Q), -1e30, jnp.float32),
-        jnp.zeros((samples, HEADS, Q), jnp.float32),
-        jnp.zeros((samples, Q, DL), jnp.float32),
-    )
-
-    def scan_step(running_state, block_index):
-        zero_index = jnp.zeros((), jnp.int32)
-        window_in = lax.dynamic_slice(
-            padded,
-            (zero_index, zero_index, block_index * BLK, zero_index),
-            (samples, channels, BLK + 2, lon_cols + 2),
-        )
-        block_features, maxima, totals, weighted = block_terms(
-            window_in, conv_weight, kv_weight, queries, BLK, lon_cols
-        )
-        return (combine_partial(running_state, (maxima, totals, weighted)), block_features)
-
-    running_state, feats = lax.scan(scan_step, initial, jnp.arange(block_count, dtype=jnp.int32))
-    features = jnp.transpose(feats, (1, 2, 0, 3, 4)).reshape(
-        samples, feats.shape[2], lat_rows, lon_cols
-    )
-    maxima, totals, weighted = running_state
-    stats = jnp.concatenate([maxima, totals], axis=1)
-    stats = jnp.transpose(stats, (0, 2, 1)).reshape(samples * Q, 2 * HEADS)
-    stats = jnp.pad(stats, ((0, 0), (0, 120)))
-    latents = reduce_all(weighted.reshape(samples * Q, DL), stats, out_weight, norm_gain)
-    latents = latents.reshape(samples, Q, DL)
-    return (features, latents)
+    xt = jnp.pad(jnp.transpose(fields, (0, 2, 1, 3)), ((0, 0), (0, 0), (0, CP - channels), (0, 0)))
+    conv_t = jnp.transpose(conv_weight, (0, 2, 1))
+    rows, cols, w2, kv2 = halo(xt, conv_t, kv_weight)
+    feats, weighted, stats = encode(xt, rows, cols, w2, kv2, queries)
+    features = feats.reshape(samples, 128, lat_rows, lon_cols)
+    latents = reduce_all(weighted, stats, out_weight, norm_gain)
+    return (features, latents.reshape(samples, Q, DL))
 
 
 def solution(mesh):

time: 156 us -> 104 us (0.67)
  Pallas kernels: 32 us -> 99.5 us
  matrix products: 60.9 us -> 0 us
  other arithmetic: 22.8 us -> 0 us
  local copies, waits for them, and re-layouts: 22.8 us -> 3.65 us
  starting transfers between devices: 8.33 us -> 0 us
  waiting for transfers between devices: 4.52 us -> 0 us
  loops' own time: 2.8 us -> 0 us
    pallas_call x0 -> x2, Pallas kernels: none -> 72.7 us  [the longest x1 60.7 us: encode(): pl.pallas_call(encode_kernel, grid=(samples, 3), out_shape=(jax.ShapeDtyp...]
    dot_general x36 -> x0, matrix products: 60.9 us -> none  [the longest x27 35.6 us: convolve_block(): jnp.einsum('fc,bcin->bfin', conv_weight[tap_index], piece, preferred_elem...]
    convert_element_type x3 -> x0, other arithmetic: 15.3 us -> none  [block_terms(): weights_bf = exponent.astype(jnp.bfloat16)]
    ppermute x4 -> x0, starting transfers between devices: 8.33 us -> none  [the longest x2 6.97 us: extended(): lax.ppermute(lax.slice_in_dim(block, block.shape[dim] - width, None, axis...]
    slice x4 -> x0, local copies, waits for them, and re-layouts: 5.34 us -> none  [the longest x1 4.01 us: extended(): lax.slice_in_dim(block, block.shape[dim] - width, None, axis=dim)]
    concatenate x1 -> x0, other arithmetic: 5.12 us -> none  [extended(): block = jnp.concatenate([low, block, high], axis=dim)]
    pallas_call x1, Pallas kernels: 32 us -> 26.8 us  [reduce_all(): pl.pallas_call(reduce_kernel, out_shape=jax.ShapeDtypeStruct((1024, 256),...]
    transpose x7 -> x0, local copies, waits for them, and re-layouts: 4.87 us -> none  [the longest x1 4.83 us: per_device(): jnp.transpose(feats, (1, 2, 0, 3, 4))]
  transfers between devices with their start and end apart: 4 -> 0, of which waited for: 1 -> 0; matrix products, arithmetic and copies ran while one was open for 3% -> 0% of each run, Pallas kernels for 0% -> 0%
where the time goes in v2:
time: 104 us
  Pallas kernels  99.5 us (96%)
  local copies, waits for them, and re-layouts  3.65 us (4%)
    pallas_call x1, Pallas kernels, encode(): pl.pallas_call(encode_kernel, grid=(samples, 3), out_shape=(jax.ShapeDtyp...  60.7 us
    pallas_call x1, Pallas kernels, reduce_all(): pl.pallas_call(reduce_kernel, out_shape=jax.ShapeDtypeStruct((1024, 256),...  26.8 us
    pallas_call x1, Pallas kernels, halo(): pl.pallas_call(halo_kernel, out_shape=(jax.ShapeDtypeStruct((2, samples,...  12 us
    unnamed x12, local copies, waits for them, and re-layouts  3.49 us

profile of v2, /device:TPU:1, one launch (start us, length us, event | category | flops | bytes accessed | tf_op | source)
XLA Modules:
  0.0 103.9 jit_solution(17283246470184605038)
XLA Ops:
  0.6 1.7 %copy.10 = bf16[4,69,24,128]{3,1,2,0:T(8,128)(2,1)S(1)} copy(bf16[4,69,24,128]{3,2,1,0:T(8,128)(2,1)} %param.6) | data formatting | bytes 3391488 | tf_op args[0]
  2.3 0.0 copy-start
  2.3 0.0 copy-start.1
  2.4 0.2 pad.4.xt_ref
  2.5 0.7 copy-done
  3.2 0.1 copy-done.1
  3.3 0.0 copy-start.3
  3.3 12.0 %shard_map.77 = (bf16[2,4,80,128]{3,2,1,0:T(8,128)(2,1)S(1)}, bf16[2,4,80,128]{3,2,1,0:T(8,128)(2,1)S(1)}, bf16[256,960]{1,0:T(8,128)(2,1)S(1)}, bf16[1024,256]{1,0:T(8,128)(2,1)S(1)}) custom-call(bf16[4,24,80,128]{3,2,1,0:T(8,128)(2,1)S(1)} %pad.4.xt_ref, bf16[9,69,128]{2,1,0:T(8,128)(2,1)S(1)} %bitcast.12, bf16[512,128]{1,0:T(8,128)(2,1)S(1)} %copy-done.1), custom_call_target="tpu_custom_call" | custom-call | tf_op jit(solution)/shard_map/pallas_call | solution.py:303
  15.4 0.0 copy-start.2
  15.4 0.0 copy-start.4
  15.4 0.0 copy-done.3
  15.4 60.7 %shard_map.78 = (bf16[4,128,12,2,128]{4,3,2,1,0:T(2,128)(2,1)}, f32[4,256,256]{2,1,0:T(8,128)S(1)}, f32[4,256,128]{2,1,0:T(8,128)S(1)}) custom-call(bf16[4,24,80,128]{3,2,1,0:T(8,128)(2,1)S(1)} %pad.4.xt_ref, bf16[2,4,80,128]{3,2,1,0:T(8,128)(2,1)S(1)} %get-tuple-element.9.rows_ref, bf16[2,4,80,128]{3,2,1,0:T(8,128)(2,1)S(1)} %get-tuple-element.10.cols_ref, ...), custom_call_target="tpu_custom_call" | custom-call | tf_op jit(solution)/shard_map/pallas_call | solution.py:391
  76.1 0.0 copy-done.2
  76.1 0.0 copy-done.4
  76.1 26.8 %shard_map.79 = f32[1024,256]{1,0:T(8,128)S(1)} custom-call(f32[2,512,256]{2,1,0:T(8,128)S(1)} %bitcast.10, f32[2,512,128]{2,1,0:T(8,128)S(1)} %bitcast.11, bf16[256,256]{1,0:T(8,128)(2,1)S(1)} %copy-done.2, f32[1,256]{1,0:T(1,128)S(1)} %bitcast.13), custom_call_target="tpu_custom_call" | custom-call | tf_op jit(solution)/shard_map/pallas_call | solution.py:135
  102.9 1.0 copy.12
Async XLA Ops:
  2.3 0.9 copy-start
  2.3 1.0 copy-start.1
  3.3 12.1 %copy-start.3 = (bf16[256,256]{1,0:T(8,128)(2,1)S(1)}, bf16[256,256]{1,0:T(8,128)(2,1)}, u32[]{:S(2)}) copy-start(bf16[256,256]{1,0:T(8,128)(2,1)} %q_ref.1) | copy-start | bytes 393220
  15.4 60.7 %copy-start.2 = (bf16[256,256]{1,0:T(8,128)(2,1)S(1)}, bf16[256,256]{1,0:T(8,128)(2,1)}, u32[]{:S(2)}) copy-start(bf16[256,256]{1,0:T(8,128)(2,1)} %ow_ref.1) | copy-start | bytes 393220
  15.4 60.7 %copy-start.4 = (f32[256]{0:T(256)S(1)}, f32[256]{0:T(256)}, u32[]{:S(2)}) copy-start(f32[256]{0:T(256)} %param.10) | copy-start | bytes 3076

commit v3 on v2

--- a/solution.py
+++ b/solution.py
@@ -161,7 +161,7 @@
 
 
 def halo_kernel(
-    xt_ref, cw_ref, kv_ref, rows_ref, cols_ref, w2_ref, kv2_ref,
+    xt_ref, cw_ref, kv_ref, rows_ref, cols_ref, w2_ref, kt_ref, vt_ref,
     edge, got, taps, send_sem, recv_sem,
 ):
     lat = lax.axis_index("lat")
@@ -254,8 +254,11 @@
     spread = jnp.where(out_at == jnp.where(in_at < 128, 2 * in_at, 2 * in_at - 255), 1.0, 0.0).astype(jnp.bfloat16)
     w2_ref[...] = lax.dot_general(spread, taps[...], NT, preferred_element_type=jnp.float32).astype(jnp.bfloat16)
     for r in range(2):
-        kv2_ref[r * 512:(r + 1) * 512] = lax.dot_general(
-            kv_ref[...], spread[:, r * 128:(r + 1) * 128], NT, preferred_element_type=jnp.float32).astype(jnp.bfloat16)
+        some = spread[:, r * 128:(r + 1) * 128]
+        kt_ref[:, r * DL:(r + 1) * DL] = lax.dot_general(
+            some, kv_ref[0:DL], NT, preferred_element_type=jnp.float32).astype(jnp.bfloat16)
+        vt_ref[r * DL:(r + 1) * DL] = lax.dot_general(
+            kv_ref[DL:2 * DL], some, NT, preferred_element_type=jnp.float32).astype(jnp.bfloat16)
 
     for c in same:
         c.wait()
@@ -306,10 +309,11 @@
             jax.ShapeDtypeStruct((2, samples, CP, 128), jnp.bfloat16),
             jax.ShapeDtypeStruct((2, samples, CP, 128), jnp.bfloat16),
             jax.ShapeDtypeStruct((256, 4 * KROW), jnp.bfloat16),
-            jax.ShapeDtypeStruct((1024, 256), jnp.bfloat16),
+            jax.ShapeDtypeStruct((256, 512), jnp.bfloat16),
+            jax.ShapeDtypeStruct((512, 256), jnp.bfloat16),
         ),
         in_specs=[vm] * 3,
-        out_specs=(vm,) * 4,
+        out_specs=(vm,) * 5,
         scratch_shapes=[
             pltpu.VMEM((2, CP, 128), jnp.bfloat16),
             pltpu.VMEM((2, 3, CP, 128), jnp.bfloat16),
@@ -322,21 +326,32 @@
     )(xt, conv_t, kv_weight)
 
 
+NBLK = 12
+TILE = 512
+
+
 def encode_kernel(
-    xt_ref, rows_ref, cols_ref, w2_ref, kv2_ref, q_ref, feat_ref, w_out, st_out,
-    x3, qs, kvs, run,
+    xt_ref, rows_ref, cols_ref, w2_ref, kt_ref, vt_ref, q_ref, feat_ref, w_out, st_out,
+    x3, qs, k_a, k_b, v_a, v_b, feat_a, feat_b, refs, tot, acc, psums, parts, sem,
 ):
-    chunk = pl.program_id(1)
+    step = pl.program_id(0)
+    ks = (k_a, k_b)
+    vs = (v_a, v_b)
+    fbuf = (feat_a, feat_b)
     lane = lax.broadcasted_iota(jnp.int32, (CP, 128), 1)
 
-    @pl.when(chunk == 0)
-    def _():
+    @pl.when(step == 0)
+    def _():
+        turned = (q_ref[...].astype(jnp.float32) * SCALE).T
+        owner = lax.broadcasted_iota(jnp.int32, (DL, Q), 0) // HD
         for h in range(HEADS):
-            qs[h] = (q_ref[:, h * HD:(h + 1) * HD].astype(jnp.float32) * SCALE).astype(jnp.bfloat16)
-        lo = cols_ref[0, 0].astype(jnp.float32)
-        hi = cols_ref[1, 0].astype(jnp.float32)
+            qs[h] = jnp.where(owner == h, turned, 0.0).astype(jnp.bfloat16)
+
+    def shifted(b):
+        lo = cols_ref[0, b].astype(jnp.float32)
+        hi = cols_ref[1, b].astype(jnp.float32)
         for i in range(26):
-            row = rows_ref[0, 0] if i == 0 else rows_ref[1, 0] if i == 25 else xt_ref[0, i - 1]
+            row = rows_ref[0, b] if i == 0 else rows_ref[1, b] if i == 25 else xt_ref[b, i - 1]
             wide = row.astype(jnp.float32)
             before = jnp.where(lane == 0, pltpu.roll(lo, (128 - i) % 128, 1), pltpu.roll(wide, 1, 1))
             after = jnp.where(lane == 127, pltpu.roll(hi, 127 - i, 1), pltpu.roll(wide, 127, 1))
@@ -344,84 +359,213 @@
             x3[i, CP:2 * CP] = row
             x3[i, 2 * CP:3 * CP] = after.astype(jnp.bfloat16)
 
-    w2 = w2_ref[...]
-    for g in range(2):
-        base = chunk * 8 + g * 4
+    def out_copy(n, slot):
+        return pltpu.make_async_copy(
+            fbuf[slot], feat_ref.at[n // 3, :, pl.ds(lax.rem(n, 3) * 4, 4)], sem.at[slot])
+
+    def conv_of(c, g):
+        base = c * 8 + g * 4
         one = x3[pl.ds(base, 4)].reshape(4 * KROW, 128)
         two = x3[pl.ds(base + 2, 4)].reshape(4 * KROW, 128)
         both = jnp.concatenate([one, two], axis=1)
-        conv = jnp.dot(w2, both, preferred_element_type=jnp.float32)
-        feats = jax.nn.gelu(conv, approximate=True).astype(jnp.bfloat16)
-        feat_ref[0, :, 2 * g] = feats[:, 0:128].reshape(128, 2, 128)
-        feat_ref[0, :, 2 * g + 1] = feats[:, 128:256].reshape(128, 2, 128)
-        kvs[:, g * 256:(g + 1) * 256] = jnp.dot(
-            kv2_ref[...], feats, preferred_element_type=jnp.float32).astype(jnp.bfloat16)
-
-    st_lane = lax.broadcasted_iota(jnp.int32, (256, 128), 1)
-    old = jnp.where(chunk == 0, jnp.where(st_lane < 4, -3e38, 0.0), run[...])
-    new = jnp.zeros((256, 128), jnp.float32)
-    for h in range(HEADS):
-        rows = slice(h * HD, (h + 1) * HD)
-        s0 = jnp.dot(qs[h], kvs[rows], preferred_element_type=jnp.float32)
-        s1 = jnp.dot(qs[h], kvs[512 + h * HD:512 + (h + 1) * HD], preferred_element_type=jnp.float32)
-        top = jnp.max(jnp.maximum(s0, s1), axis=1, keepdims=True)
-        before = old[:, h:h + 1]
-        peak = jnp.maximum(before, top)
-        mine = jnp.exp(top - peak)
-        keep = jnp.exp(before - peak)
-        p0 = jnp.exp(s0 - top)
-        p1 = jnp.exp(s1 - top)
-        total = jnp.sum(p0 + p1, axis=1, keepdims=True)
-        v0 = kvs[256 + h * HD:256 + (h + 1) * HD]
-        v1 = kvs[768 + h * HD:768 + (h + 1) * HD]
-        part = (lax.dot_general(p0.astype(jnp.bfloat16), v0, NT, preferred_element_type=jnp.float32)
-                + lax.dot_general(p1.astype(jnp.bfloat16), v1, NT, preferred_element_type=jnp.float32))
-        sofar = jnp.where(chunk == 0, 0.0, w_out[0, :, rows])
-        w_out[0, :, rows] = sofar * keep + part * mine
-        total = old[:, 4 + h:5 + h] * keep + total * mine
-        new = jnp.where(st_lane == h, peak, jnp.where(st_lane == 4 + h, total, new))
-    run[...] = new
-    st_out[0] = new
-
-
-def encode(xt, rows, cols, w2, kv2, queries):
+        conv = jnp.dot(w2_ref[...], both, preferred_element_type=jnp.float32)
+        return jax.nn.gelu(conv, approximate=True).astype(jnp.bfloat16)
+
+    def keep_features(feats, slot, g):
+        fbuf[slot][:, 2 * g] = feats[:, 0:128].reshape(128, 2, 128)
+        fbuf[slot][:, 2 * g + 1] = feats[:, 128:256].reshape(128, 2, 128)
+
+    def project(feats, slot, g):
+        turned = feats.T
+        values = jnp.dot(vt_ref[...], feats, preferred_element_type=jnp.float32).astype(jnp.bfloat16)
+        keys = jnp.dot(turned, kt_ref[...], preferred_element_type=jnp.float32).astype(jnp.bfloat16)
+        for r in range(2):
+            at = r * 512 + g * 256
+            vs[slot][:, at:at + 256] = values[r * DL:(r + 1) * DL]
+            ks[slot][at:at + 256] = keys[:, r * DL:(r + 1) * DL]
+
+    def weigh(slot, h, ref, psum, part):
+        for n in range(0, 1024, TILE):
+            s = jnp.dot(ks[slot][n:n + TILE], qs[h], preferred_element_type=jnp.float32)
+            p = jnp.exp(s - ref)
+            psum = psum + jnp.sum(p.reshape(TILE // 8, 8, Q), axis=0)
+            part = part + jnp.dot(
+                vs[slot][h * HD:(h + 1) * HD, n:n + TILE], p.astype(jnp.bfloat16), preferred_element_type=jnp.float32)
+        return psum, part
+
+    def score(slot, h, n):
+        return jnp.dot(ks[slot][n:n + TILE], qs[h], preferred_element_type=jnp.float32)
+
+    def absorb(slot, state, s, h, n):
+        p = jnp.exp(s - refs[h])
+        psum = jnp.sum(p.reshape(TILE // 8, 8, Q), axis=0)
+        part = jnp.dot(
+            vs[slot][h * HD:(h + 1) * HD, n:n + TILE], p.astype(jnp.bfloat16), preferred_element_type=jnp.float32)
+        if n > 0:
+            psum = psum + state[h][0]
+            part = part + state[h][1]
+        state[h] = (psum, part)
+        if n + TILE == 1024:
+            psums[h] = psum
+            parts[h] = part
+
+    def head(slot, h):
+        psum, part = weigh(slot, h, refs[h], jnp.zeros((8, Q), jnp.float32), jnp.zeros((HD, Q), jnp.float32))
+        psums[h] = psum
+        parts[h] = part
+
+    def restart(slot):
+        for h in range(HEADS):
+            s = jnp.dot(ks[slot][0:128], qs[h], preferred_element_type=jnp.float32)
+            refs[h] = jnp.max(s, axis=0, keepdims=True)
+            tot[h] = jnp.zeros((8, Q), jnp.float32)
+            acc[h] = jnp.zeros((HD, Q), jnp.float32)
+
+    def settle(slot, n):
+        high = psums[0]
+        for h in range(1, HEADS):
+            high = jnp.maximum(high, psums[h])
+        fine = jnp.max(high) < 1e20
+
+        @pl.when(fine)
+        def _():
+            for h in range(HEADS):
+                tot[h] += psums[h]
+                acc[h] += parts[h]
+
+        @pl.when(jnp.logical_not(fine))
+        def _():
+            for h in range(HEADS):
+                top = refs[h]
+                for n in range(0, 1024, TILE):
+                    s = jnp.dot(ks[slot][n:n + TILE], qs[h], preferred_element_type=jnp.float32)
+                    top = jnp.maximum(top, jnp.max(s, axis=0, keepdims=True))
+                keep = jnp.exp(refs[h] - top)
+                psum, part = weigh(slot, h, top, tot[h] * keep, acc[h] * keep)
+                tot[h] = psum
+                acc[h] = part
+                refs[h] = top
+
+        @pl.when(lax.rem(n, 3) == 2)
+        def _():
+            b = n // 3
+            line = lax.broadcasted_iota(jnp.int32, (128, Q), 0)
+            new = jnp.zeros((128, Q), jnp.float32)
+            for h in range(HEADS):
+                total = jnp.sum(tot[h], axis=0, keepdims=True)
+                new = jnp.where(line == h, refs[h], jnp.where(line == 4 + h, total, new))
+            st_out[b] = new.T
+            w_out[b] = acc[...].reshape(DL, Q).T
+
+    def half(n, slot):
+        real = jnp.minimum(n, NBLK - 1)
+        c = lax.rem(real, 3)
+        other = 1 - slot
+
+        @pl.when(jnp.logical_and(c == 0, n < NBLK))
+        def _():
+            shifted(n // 3)
+
+        @pl.when(n >= 2)
+        def _():
+            out_copy(n - 2, slot).wait()
+
+        @pl.when(jnp.logical_and(n > 0, lax.rem(n - 1, 3) == 0))
+        def _():
+            restart(other)
+
+        jobs = [(h, n) for h in range(HEADS) for n in range(0, 1024, TILE)]
+        ahead = score(other, *jobs[0])
+        state = {}
+        now = ahead
+        ahead = score(other, *jobs[1])
+        f0 = conv_of(c, 0)
+        absorb(other, state, now, *jobs[0])
+        now = ahead
+        ahead = score(other, *jobs[2])
+        absorb(other, state, now, *jobs[1])
+        now = ahead
+        ahead = score(other, *jobs[3])
+        keep_features(f0, slot, 0)
+        project(f0, slot, 0)
+        absorb(other, state, now, *jobs[2])
+        now = ahead
+        ahead = score(other, *jobs[4])
+        absorb(other, state, now, *jobs[3])
+        now = ahead
+        ahead = score(other, *jobs[5])
+        f1 = conv_of(c, 1)
+        absorb(other, state, now, *jobs[4])
+        now = ahead
+        ahead = score(other, *jobs[6])
+        absorb(other, state, now, *jobs[5])
+        now = ahead
+        ahead = score(other, *jobs[7])
+        keep_features(f1, slot, 1)
+        project(f1, slot, 1)
+        absorb(other, state, now, *jobs[6])
+        now = ahead
+        absorb(other, state, now, *jobs[7])
+
+        @pl.when(n < NBLK)
+        def _():
+            out_copy(n, slot).start()
+
+        @pl.when(n > 0)
+        def _():
+            settle(other, n - 1)
+
+    half(2 * step, 0)
+
+    @pl.when(step < NBLK // 2)
+    def _():
+        half(2 * step + 1, 1)
+
+    @pl.when(step == NBLK // 2)
+    def _():
+        out_copy(NBLK - 1, 1).wait()
+
+
+def encode(xt, rows, cols, w2, kt, vt, queries):
     samples = xt.shape[0]
     whole = pl.BlockSpec(memory_space=pltpu.VMEM)
-    side = pl.BlockSpec((2, 1, CP, 128), lambda b, c: (0, b, 0, 0))
     return pl.pallas_call(
         encode_kernel,
-        grid=(samples, 3),
+        grid=(NBLK // 2 + 1,),
         out_shape=(
             jax.ShapeDtypeStruct((samples, 128, 12, 2, 128), jnp.bfloat16),
             jax.ShapeDtypeStruct((samples, Q, DL), jnp.float32),
             jax.ShapeDtypeStruct((samples, Q, 128), jnp.float32),
         ),
-        in_specs=[
-            pl.BlockSpec((1, 24, CP, 128), lambda b, c: (b, 0, 0, 0)),
-            side, side, whole, whole, whole,
-        ],
-        out_specs=(
-            pl.BlockSpec((1, 128, 4, 2, 128), lambda b, c: (b, 0, c, 0, 0)),
-            pl.BlockSpec((1, Q, DL), lambda b, c: (b, 0, 0)),
-            pl.BlockSpec((1, Q, 128), lambda b, c: (b, 0, 0)),
-        ),
+        in_specs=[whole] * 7,
+        out_specs=(pl.BlockSpec(memory_space=pl.ANY), whole, whole),
         scratch_shapes=[
             pltpu.VMEM((26, KROW, 128), jnp.bfloat16),
-            pltpu.VMEM((HEADS, Q, HD), jnp.bfloat16),
-            pltpu.VMEM((1024, 512), jnp.bfloat16),
-            pltpu.VMEM((Q, 128), jnp.float32),
+            pltpu.VMEM((HEADS, DL, Q), jnp.bfloat16),
+            pltpu.VMEM((1024, DL), jnp.bfloat16),
+            pltpu.VMEM((1024, DL), jnp.bfloat16),
+            pltpu.VMEM((DL, 1024), jnp.bfloat16),
+            pltpu.VMEM((DL, 1024), jnp.bfloat16),
+            pltpu.VMEM((128, 4, 2, 128), jnp.bfloat16),
+            pltpu.VMEM((128, 4, 2, 128), jnp.bfloat16),
+            pltpu.VMEM((HEADS, 1, Q), jnp.float32),
+            pltpu.VMEM((HEADS, 8, Q), jnp.float32),
+            pltpu.VMEM((HEADS, HD, Q), jnp.float32),
+            pltpu.VMEM((HEADS, 8, Q), jnp.float32),
+            pltpu.VMEM((HEADS, HD, Q), jnp.float32),
+            pltpu.SemaphoreType.DMA((2,)),
         ],
         compiler_params=pltpu.CompilerParams(
-            dimension_semantics=("arbitrary", "arbitrary"), vmem_limit_bytes=48 * 1024 * 1024),
-    )(xt, rows, cols, w2, kv2, queries)
+            dimension_semantics=("arbitrary",), vmem_limit_bytes=40 * 1024 * 1024),
+    )(xt, rows, cols, w2, kt, vt, queries)
 
 
 def per_device(fields, conv_weight, kv_weight, out_weight, norm_gain, queries):
     samples, channels, lat_rows, lon_cols = fields.shape
     xt = jnp.pad(jnp.transpose(fields, (0, 2, 1, 3)), ((0, 0), (0, 0), (0, CP - channels), (0, 0)))
     conv_t = jnp.transpose(conv_weight, (0, 2, 1))
-    rows, cols, w2, kv2 = halo(xt, conv_t, kv_weight)
-    feats, weighted, stats = encode(xt, rows, cols, w2, kv2, queries)
+    rows, cols, w2, kt, vt = halo(xt, conv_t, kv_weight)
+    feats, weighted, stats = encode(xt, rows, cols, w2, kt, vt, queries)
     features = feats.reshape(samples, 128, lat_rows, lon_cols)
     latents = reduce_all(weighted, stats, out_weight, norm_gain)
     return (features, latents.reshape(samples, Q, DL))

time: 104 us -> 105 us (level)
  Pallas kernels: 99.5 us -> 101 us
    pallas_call x1, Pallas kernels: 26.8 us -> 29.5 us  [reduce_all(): pl.pallas_call(reduce_kernel, out_shape=jax.ShapeDtypeStruct((1024, 256),...]
    pallas_call x1, Pallas kernels: 60.7 us -> 59.1 us  [encode(): pl.pallas_call(encode_kernel, grid=(NBLK // 2 + 1,), out_shape=(jax.Shape...]
where the time goes in v3:
time: 105 us
  Pallas kernels  101 us (96%)
  local copies, waits for them, and re-layouts  3.65 us (3%)
    pallas_call x1, Pallas kernels, encode(): pl.pallas_call(encode_kernel, grid=(NBLK // 2 + 1,), out_shape=(jax.Shape...  59.1 us
    pallas_call x1, Pallas kernels, reduce_all(): pl.pallas_call(reduce_kernel, out_shape=jax.ShapeDtypeStruct((1024, 256),...  29.5 us
    pallas_call x1, Pallas kernels, halo(): pl.pallas_call(halo_kernel, out_shape=(jax.ShapeDtypeStruct((2, samples,...  12 us
    unnamed x12, local copies, waits for them, and re-layouts  3.49 us

profile of v3, /device:TPU:1, one launch (start us, length us, event | category | flops | bytes accessed | tf_op | source)
XLA Modules:
  0.0 105.0 jit_solution(6076595701725847469)
XLA Ops:
  0.6 1.7 %copy.10 = bf16[4,69,24,128]{3,1,2,0:T(8,128)(2,1)S(1)} copy(bf16[4,69,24,128]{3,2,1,0:T(8,128)(2,1)} %param.6) | data formatting | bytes 3391488 | tf_op args[0]
  2.3 0.0 copy-start
  2.3 0.0 copy-start.1
  2.4 0.2 pad.4.xt_ref
  2.5 0.7 copy-done
  3.2 0.1 copy-done.1
  3.3 0.0 copy-start.3
  3.3 12.0 %shard_map.77 = (bf16[2,4,80,128]{3,2,1,0:T(8,128)(2,1)S(1)}, bf16[2,4,80,128]{3,2,1,0:T(8,128)(2,1)S(1)}, bf16[256,960]{1,0:T(8,128)(2,1)S(1)}, bf16[256,512]{1,0:T(8,128)(2,1)S(1)}, bf16[512,256]{1,0:T(8,128)(2,1)S(1)}) custom-call(bf16[4,24,80,128]{3,2,1,0:T(8,128)(2,1)S(1)} %pad.4.xt_ref, bf16[9,69,128]{2,1,0:T(8,128)(2,1)S(1)} %bitcast.12, ...), custom_call_target="tpu_custom_call" | custom-call | tf_op jit(solution)/shard_map/pallas_call | solution.py:306
  15.4 0.0 copy-start.2
  15.4 0.0 copy-start.4
  15.4 0.0 copy-done.3
  15.4 59.1 %shard_map.78 = (bf16[4,128,12,2,128]{4,3,2,1,0:T(2,128)(2,1)}, f32[4,256,256]{2,1,0:T(8,128)S(1)}, f32[4,256,128]{2,1,0:T(8,128)S(1)}) custom-call(bf16[4,24,80,128]{3,2,1,0:T(8,128)(2,1)S(1)} %pad.4.xt_ref, bf16[2,4,80,128]{3,2,1,0:T(8,128)(2,1)S(1)} %get-tuple-element.10.rows_ref, bf16[2,4,80,128]{3,2,1,0:T(8,128)(2,1)S(1)} %get-tuple-element.11.cols_ref, ...), custom_call_target="tpu_custom_call" | custom-call | tf_op jit(solution)/shard_map/pallas_call | solution.py:532
  74.5 0.0 copy-done.2
  74.6 0.0 copy-done.4
  74.6 29.5 %shard_map.79 = f32[1024,256]{1,0:T(8,128)S(1)} custom-call(f32[2,512,256]{2,1,0:T(8,128)S(1)} %bitcast.10, f32[2,512,128]{2,1,0:T(8,128)S(1)} %bitcast.11, bf16[256,256]{1,0:T(8,128)(2,1)S(1)} %copy-done.2, f32[1,256]{1,0:T(1,128)S(1)} %bitcast.13), custom_call_target="tpu_custom_call" | custom-call | tf_op jit(solution)/shard_map/pallas_call | solution.py:135
  104.1 1.0 copy.12
Async XLA Ops:
  2.3 0.9 copy-start
  2.3 1.0 copy-start.1
  3.3 12.1 %copy-start.3 = (bf16[256,256]{1,0:T(8,128)(2,1)S(1)}, bf16[256,256]{1,0:T(8,128)(2,1)}, u32[]{:S(2)}) copy-start(bf16[256,256]{1,0:T(8,128)(2,1)} %q_ref.1) | copy-start | bytes 393220
  15.4 59.2 %copy-start.2 = (bf16[256,256]{1,0:T(8,128)(2,1)S(1)}, bf16[256,256]{1,0:T(8,128)(2,1)}, u32[]{:S(2)}) copy-start(bf16[256,256]{1,0:T(8,128)(2,1)} %ow_ref.1) | copy-start | bytes 393220
  15.4 59.2 %copy-start.4 = (f32[256]{0:T(256)S(1)}, f32[256]{0:T(256)}, u32[]{:S(2)}) copy-start(f32[256]{0:T(256)} %param.10) | copy-start | bytes 3076

commit v4 on v3

--- a/solution.py
+++ b/solution.py
@@ -17,7 +17,7 @@
 
 def reduce_kernel(
     w_ref, st_ref, ow_ref, gain_ref, out_ref,
-    half_w, half_st, msg, recv, own, gath,
+    half_w, half_st, msg, recv, gath,
     sem_a, sem_b, sem_c,
 ):
     lat = lax.axis_index("lat")
@@ -40,40 +40,44 @@
     lax.fori_loop(1, NCHIP, greet, 0)
     pl.semaphore_wait(barrier, NCHIP)
 
-    give = 1 - core
-    cw = pltpu.make_async_remote_copy(
-        w_ref.at[give], half_w, sem_a.at[0], sem_a.at[1], device_id=(lat, partner), device_id_type=MESH)
+    give = 2 - 2 * core
+    keep = 2 * core
     cs = pltpu.make_async_remote_copy(
-        st_ref.at[give], half_st, sem_a.at[2], sem_a.at[3], device_id=(lat, partner), device_id_type=MESH)
+        st_ref.at[pl.ds(give, 2)], half_st, sem_a.at[0], sem_a.at[1],
+        device_id=(lat, partner), device_id_type=MESH)
+    cw = [
+        pltpu.make_async_remote_copy(
+            w_ref.at[give + i], half_w.at[i], sem_a.at[2 + 2 * i], sem_a.at[3 + 2 * i],
+            device_id=(lat, partner), device_id_type=MESH)
+        for i in range(2)
+    ]
     cs.start()
-    cw.start()
-    cs.wait()
-    cw.wait()
-
-    s1 = st_ref[core]
-    s2 = half_st[...]
-    peak = jnp.maximum(s1, s2)
-    f1 = jnp.exp(s1 - peak)
-    f2 = jnp.exp(s2 - peak)
-    lane = lax.broadcasted_iota(jnp.int32, (512, 128), 1)
-    t1 = pltpu.roll(s1, 124, 1)
-    t2 = pltpu.roll(s2, 124, 1)
-    tot = t1 * f1 + t2 * f2
-    for h in range(4):
-        cols = slice(h * 64, h * 64 + 64)
-        val = w_ref[core, :, cols] * f1[:, h:h + 1] + half_w[:, cols] * f2[:, h:h + 1]
-        msg[:, :, cols] = val.reshape(NCHIP, ROWS, 64).astype(jnp.bfloat16)
+    for c in cw:
+        c.start()
 
     def limbs(v):
         a = v.astype(jnp.bfloat16).astype(jnp.float32)
         b = (v - a).astype(jnp.bfloat16).astype(jnp.float32)
-        return a, b, v - a - b
-
-    m0, m1, m2 = limbs(jnp.where(lane < 4, peak, 0.0))
-    q0, q1, q2 = limbs(jnp.where(lane < 4, tot, 0.0))
-    packed = (m0 + pltpu.roll(m1, 4, 1) + pltpu.roll(m2, 8, 1)
-              + pltpu.roll(q0, 12, 1) + pltpu.roll(q1, 16, 1) + pltpu.roll(q2, 20, 1))
-    msg[:, :, 256:384] = packed.reshape(NCHIP, ROWS, 128).astype(jnp.bfloat16)
+        return [a, b, v - a - b]
+
+    cs.wait()
+    for i in range(2):
+        s1 = st_ref[keep + i]
+        s2 = half_st[i]
+        peak = jnp.maximum(s1[0:4], s2[0:4])
+        f1 = jnp.exp(s1[0:4] - peak)
+        f2 = jnp.exp(s2[0:4] - peak)
+        total = s1[4:8] * f1 + s2[4:8] * f2
+        cw[i].wait()
+        for h in range(HEADS):
+            line = slice(h, h + 1)
+            rows = slice(h * HD, (h + 1) * HD)
+            value = w_ref[keep + i, rows] * f1[line] + half_w[i, rows] * f2[line]
+            first = i * 32 + h * 8
+            msg[first:first + 8, 0:ROWS] = value.reshape(8, ROWS, Q).astype(jnp.bfloat16)
+            extra = jnp.concatenate(
+                limbs(peak[line]) + limbs(total[line]) + [jnp.zeros((2, Q), jnp.float32)], axis=0)
+            msg[first:first + 8, ROWS:2 * ROWS] = jnp.broadcast_to(extra[None], (8, ROWS, Q)).astype(jnp.bfloat16)
 
     def scatter(k, _):
         c = lax.rem(chip + k, NCHIP)
@@ -82,32 +86,22 @@
         return 0
 
     lax.fori_loop(1, NCHIP, scatter, 0)
-    own[...] = msg[chip]
+    own = msg[chip].astype(jnp.float32)
     pltpu.make_async_copy(recv, recv, sem_b.at[1]).wait()
 
-    def stats(v):
-        m = v + pltpu.roll(v, 124, 1) + pltpu.roll(v, 120, 1)
-        t = pltpu.roll(v, 116, 1) + pltpu.roll(v, 112, 1) + pltpu.roll(v, 108, 1)
-        return m, t
-
-    def unpack(buf):
-        return buf.astype(jnp.float32)
-
-    all_st = jnp.concatenate([recv[:, :, 256:384].astype(jnp.float32), own[:, 256:384].astype(jnp.float32)[None]], axis=0)
-    am, at = stats(all_st.reshape(512, 128))
-    am = am.reshape(NCHIP, ROWS, 128)
-    at = at.reshape(NCHIP, ROWS, 128)
-    top = jnp.max(am, axis=0)
-    fac = jnp.exp(am - top[None])
-    total = jnp.sum(fac * at, axis=0)
-    for h in range(4):
-        cols = slice(h * 64, h * 64 + 64)
-        acc = (jnp.sum(recv[:, :, cols].astype(jnp.float32) * fac[:63, :, h:h + 1], axis=0)
-               + own[:, cols].astype(jnp.float32) * fac[63, :, h:h + 1])
-        gath[core * NCHIP + chip, :, cols] = (acc / total[:, h:h + 1]).astype(jnp.bfloat16)
-    pltpu.make_async_copy(recv, recv, sem_b.at[0]).wait()
-
+    got = recv[...].astype(jnp.float32)
+    extra = got[:, ROWS:2 * ROWS]
+    m = extra[:, 0:1] + extra[:, 1:2] + extra[:, 2:3]
+    t = extra[:, 3:4] + extra[:, 4:5] + extra[:, 5:6]
+    own_m = own[8:9] + own[9:10] + own[10:11]
+    own_t = own[11:12] + own[12:13] + own[13:14]
+    top = jnp.maximum(jnp.max(m, axis=0), own_m)
+    fac = jnp.exp(m - top[None])
+    own_fac = jnp.exp(own_m - top)
+    total = jnp.sum(fac * t, axis=0) + own_fac * own_t
+    summed = jnp.sum(got[:, 0:ROWS] * fac, axis=0) + own[0:ROWS] * own_fac
     mine = core * NCHIP + chip
+    gath[mine] = (summed / total).astype(jnp.bfloat16)
 
     def spread(k, _):
         pltpu.make_async_remote_copy(
@@ -115,43 +109,50 @@
         return 0
 
     lax.fori_loop(1, NCHIP, spread, 0)
+    pltpu.make_async_copy(recv, recv, sem_b.at[0]).wait()
     size = gath.at[pl.ds(0, NCHIP - 1)]
     pltpu.make_async_copy(size, size, sem_c.at[1]).wait()
-    pltpu.make_async_copy(size, size, sem_c.at[0]).wait()
     block = gath.at[pl.ds(core * NCHIP, NCHIP)]
     cg = pltpu.make_async_remote_copy(
         block, block, sem_c.at[2], sem_c.at[3], device_id=(lat, partner), device_id_type=MESH)
     cg.start()
+
+    def finish(b):
+        att = gath[pl.ds(b * 32, 32)].astype(jnp.float32).reshape(DL, Q).T.astype(jnp.bfloat16)
+        proj = jnp.dot(att, ow_ref[...], preferred_element_type=jnp.float32)
+        out_ref[b] = (
+            proj * lax.rsqrt(jnp.mean(proj * proj, axis=-1, keepdims=True) + 1e-06) * gain_ref[...]
+        )
+
+    finish(keep)
+    finish(keep + 1)
     cg.wait()
-    att = gath[...].astype(jnp.float32).reshape(1024, 256).astype(jnp.bfloat16)
-    proj = jnp.dot(att, ow_ref[...], preferred_element_type=jnp.float32)
-    out_ref[...] = (
-        proj * lax.rsqrt(jnp.mean(proj * proj, axis=-1, keepdims=True) + 1e-06) * gain_ref[...]
-    )
+    finish(give)
+    finish(give + 1)
+    pltpu.make_async_copy(size, size, sem_c.at[0]).wait()
 
 
 def reduce_all(weighted, stats, out_weight, norm_gain):
     vm = pl.BlockSpec(memory_space=pltpu.VMEM)
     return pl.pallas_call(
         reduce_kernel,
-        out_shape=jax.ShapeDtypeStruct((1024, 256), jnp.float32),
+        out_shape=jax.ShapeDtypeStruct((4, Q, DL), jnp.float32),
         in_specs=[vm] * 4,
         out_specs=vm,
         scratch_shapes=[
-            pltpu.VMEM((512, 256), jnp.float32),
-            pltpu.VMEM((512, 128), jnp.float32),
-            pltpu.VMEM((NCHIP, ROWS, 384), jnp.bfloat16),
-            pltpu.VMEM((NCHIP - 1, ROWS, 384), jnp.bfloat16),
-            pltpu.VMEM((ROWS, 384), jnp.bfloat16),
-            pltpu.VMEM((2 * NCHIP, ROWS, 256), jnp.bfloat16),
-            pltpu.SemaphoreType.DMA((4,)),
+            pltpu.VMEM((2, DL, Q), jnp.float32),
+            pltpu.VMEM((2, 8, Q), jnp.float32),
+            pltpu.VMEM((NCHIP, 2 * ROWS, Q), jnp.bfloat16),
+            pltpu.VMEM((NCHIP - 1, 2 * ROWS, Q), jnp.bfloat16),
+            pltpu.VMEM((2 * NCHIP, ROWS, Q), jnp.bfloat16),
+            pltpu.SemaphoreType.DMA((6,)),
             pltpu.SemaphoreType.DMA((2,)),
             pltpu.SemaphoreType.DMA((4,)),
         ],
         compiler_params=pltpu.CompilerParams(
             collective_id=1, has_side_effects=True, vmem_limit_bytes=32 * 1024 * 1024
         ),
-    )(weighted.reshape(2, 512, 256), stats.reshape(2, 512, 128), out_weight, norm_gain.reshape(1, 256))
+    )(weighted, stats, out_weight, norm_gain.reshape(1, DL))
 
 
 CP = 80
@@ -197,8 +198,9 @@
         for i in range(24):
             at = b * 24 + i
             row = xt_ref[b, i].astype(jnp.float32)
-            last = jnp.where(lane == at, pltpu.roll(row, (at + 1) % 128, 1), last)
-            first = jnp.where(lane == at, pltpu.roll(row, at, 1), first)
+            turned = pltpu.roll(row, at + 1, 1)
+            last = jnp.where(lane == at, turned, last)
+            first = jnp.where(lane == at + 1, turned, first)
     edge[0] = last.astype(jnp.bfloat16)
     edge[1] = first.astype(jnp.bfloat16)
 
@@ -294,9 +296,10 @@
         above = got[side, 1].astype(jnp.float32)
         below = got[side, 2].astype(jnp.float32)
         for b in range(4):
-            value = pltpu.roll(mid, (129 - b * 24) % 128, 1)
-            value = jnp.where(lane == 0, pltpu.roll(above, (128 - b * 24 - 23) % 128, 1), value)
-            value = jnp.where(lane == 25, pltpu.roll(below, (128 + 25 - b * 24) % 128, 1), value)
+            at = b * 24 + side
+            value = pltpu.roll(mid, (129 - at) % 128, 1)
+            value = jnp.where(lane == 0, pltpu.roll(above, (128 - at - 23) % 128, 1), value)
+            value = jnp.where(lane == 25, pltpu.roll(below, (128 + 25 - at) % 128, 1), value)
             cols_ref[side, b] = value.astype(jnp.bfloat16)
 
 
@@ -347,26 +350,37 @@
         for h in range(HEADS):
             qs[h] = jnp.where(owner == h, turned, 0.0).astype(jnp.bfloat16)
 
-    def shifted(b):
-        lo = cols_ref[0, b].astype(jnp.float32)
-        hi = cols_ref[1, b].astype(jnp.float32)
-        for i in range(26):
-            row = rows_ref[0, b] if i == 0 else rows_ref[1, b] if i == 25 else xt_ref[b, i - 1]
-            wide = row.astype(jnp.float32)
-            before = jnp.where(lane == 0, pltpu.roll(lo, (128 - i) % 128, 1), pltpu.roll(wide, 1, 1))
-            after = jnp.where(lane == 127, pltpu.roll(hi, 127 - i, 1), pltpu.roll(wide, 127, 1))
-            x3[i, 0:CP] = before.astype(jnp.bfloat16)
-            x3[i, CP:2 * CP] = row
-            x3[i, 2 * CP:3 * CP] = after.astype(jnp.bfloat16)
+    def put_row(slot, i, row, lo, hi):
+        before = jnp.where(lane == 0, lo, pltpu.roll(row, 1, 1))
+        after = jnp.where(lane == 127, hi, pltpu.roll(row, 127, 1))
+        x3[slot, i, 0:CP] = before
+        x3[slot, i, CP:2 * CP] = row
+        x3[slot, i, 2 * CP:3 * CP] = after
+
+    def outer_rows(b, slot):
+        lo = cols_ref[0, b]
+        hi = cols_ref[1, b]
+        put_row(slot, 0, rows_ref[0, b], lo, pltpu.roll(hi, 127, 1))
+        put_row(slot, 25, rows_ref[1, b], pltpu.roll(lo, 103, 1), pltpu.roll(hi, 102, 1))
+
+    def inner_rows(b, slot, c):
+        lo = pltpu.roll(cols_ref[0, b], 128 - 8 * c, 1) if isinstance(c, int) and c > 0 else cols_ref[0, b]
+        hi = pltpu.roll(cols_ref[1, b], 128 - 8 * c, 1) if isinstance(c, int) and c > 0 else cols_ref[1, b]
+        if not isinstance(c, int):
+            lo = pltpu.roll(lo.astype(jnp.float32), lax.rem(128 - 8 * c, 128), 1).astype(jnp.bfloat16)
+            hi = pltpu.roll(hi.astype(jnp.float32), lax.rem(128 - 8 * c, 128), 1).astype(jnp.bfloat16)
+        for j in range(8):
+            put_row(slot, 8 * c + 1 + j, xt_ref[b, 8 * c + j],
+                    pltpu.roll(lo, 127 - j, 1), pltpu.roll(hi, 126 - j, 1))
 
     def out_copy(n, slot):
         return pltpu.make_async_copy(
             fbuf[slot], feat_ref.at[n // 3, :, pl.ds(lax.rem(n, 3) * 4, 4)], sem.at[slot])
 
-    def conv_of(c, g):
+    def conv_of(b, c, g):
         base = c * 8 + g * 4
-        one = x3[pl.ds(base, 4)].reshape(4 * KROW, 128)
-        two = x3[pl.ds(base + 2, 4)].reshape(4 * KROW, 128)
+        one = x3[lax.rem(b, 2), pl.ds(base, 4)].reshape(4 * KROW, 128)
+        two = x3[lax.rem(b, 2), pl.ds(base + 2, 4)].reshape(4 * KROW, 128)
         both = jnp.concatenate([one, two], axis=1)
         conv = jnp.dot(w2_ref[...], both, preferred_element_type=jnp.float32)
         return jax.nn.gelu(conv, approximate=True).astype(jnp.bfloat16)
@@ -449,22 +463,22 @@
         @pl.when(lax.rem(n, 3) == 2)
         def _():
             b = n // 3
-            line = lax.broadcasted_iota(jnp.int32, (128, Q), 0)
-            new = jnp.zeros((128, Q), jnp.float32)
+            line = lax.broadcasted_iota(jnp.int32, (8, Q), 0)
+            new = jnp.zeros((8, Q), jnp.float32)
             for h in range(HEADS):
                 total = jnp.sum(tot[h], axis=0, keepdims=True)
                 new = jnp.where(line == h, refs[h], jnp.where(line == 4 + h, total, new))
-            st_out[b] = new.T
-            w_out[b] = acc[...].reshape(DL, Q).T
-
-    def half(n, slot):
-        real = jnp.minimum(n, NBLK - 1)
-        c = lax.rem(real, 3)
+            st_out[b] = new
+            w_out[b] = acc[...].reshape(DL, Q)
+
+    def half(n, slot, begin, end):
+        b = n // 3
+        c = lax.rem(n, 3)
         other = 1 - slot
 
         @pl.when(jnp.logical_and(c == 0, n < NBLK))
         def _():
-            shifted(n // 3)
+            outer_rows(b, lax.rem(b, 2))
 
         @pl.when(n >= 2)
         def _():
@@ -474,38 +488,90 @@
         def _():
             restart(other)
 
-        jobs = [(h, n) for h in range(HEADS) for n in range(0, 1024, TILE)]
-        ahead = score(other, *jobs[0])
-        state = {}
-        now = ahead
-        ahead = score(other, *jobs[1])
-        f0 = conv_of(c, 0)
-        absorb(other, state, now, *jobs[0])
-        now = ahead
-        ahead = score(other, *jobs[2])
-        absorb(other, state, now, *jobs[1])
-        now = ahead
-        ahead = score(other, *jobs[3])
-        keep_features(f0, slot, 0)
-        project(f0, slot, 0)
-        absorb(other, state, now, *jobs[2])
-        now = ahead
-        ahead = score(other, *jobs[4])
-        absorb(other, state, now, *jobs[3])
-        now = ahead
-        ahead = score(other, *jobs[5])
-        f1 = conv_of(c, 1)
-        absorb(other, state, now, *jobs[4])
-        now = ahead
-        ahead = score(other, *jobs[6])
-        absorb(other, state, now, *jobs[5])
-        now = ahead
-        ahead = score(other, *jobs[7])
-        keep_features(f1, slot, 1)
-        project(f1, slot, 1)
-        absorb(other, state, now, *jobs[6])
-        now = ahead
-        absorb(other, state, now, *jobs[7])
+        if begin:
+            @pl.when(n == 0)
+            def _():
+                for part in range(3):
+                    inner_rows(0, 0, part)
+                inner_rows(1, 1, 0)
+                f0 = conv_of(b, c, 0)
+                f1 = conv_of(b, c, 1)
+                keep_features(f0, slot, 0)
+                project(f0, slot, 0)
+                keep_features(f1, slot, 1)
+                project(f1, slot, 1)
+
+        def mixed():
+            after = jnp.minimum(b + 1, xt_ref.shape[0] - 1)
+            next_slot = lax.rem(b + 1, 2)
+            jobs = [(h, n) for h in range(HEADS) for n in range(0, 1024, TILE)]
+            ahead = score(other, *jobs[0])
+            state = {}
+            now = ahead
+            ahead = score(other, *jobs[1])
+            f0 = conv_of(b, c, 0)
+            absorb(other, state, now, *jobs[0])
+            now = ahead
+            ahead = score(other, *jobs[2])
+            f1 = conv_of(b, c, 1)
+            inner_rows(after, next_slot, c)
+            absorb(other, state, now, *jobs[1])
+            now = ahead
+            ahead = score(other, *jobs[3])
+            absorb(other, state, now, *jobs[2])
+            now = ahead
+            ahead = score(other, *jobs[4])
+            keep_features(f0, slot, 0)
+            project(f0, slot, 0)
+            absorb(other, state, now, *jobs[3])
+            now = ahead
+            ahead = score(other, *jobs[5])
+            absorb(other, state, now, *jobs[4])
+            now = ahead
+            ahead = score(other, *jobs[6])
+            keep_features(f1, slot, 1)
+            project(f1, slot, 1)
+            absorb(other, state, now, *jobs[5])
+            now = ahead
+            ahead = score(other, *jobs[7])
+            absorb(other, state, now, *jobs[6])
+            now = ahead
+            absorb(other, state, now, *jobs[7])
+
+        if begin or end:
+            pl.when(jnp.logical_and(n > 0, n < NBLK))(mixed)
+        else:
+            mixed()
+
+        if end:
+            @pl.when(n == NBLK)
+            def _():
+                jobs = [(h, n) for h in range(HEADS) for n in range(0, 1024, TILE)]
+                ahead = score(other, *jobs[0])
+                state = {}
+                now = ahead
+                ahead = score(other, *jobs[1])
+                absorb(other, state, now, *jobs[0])
+                now = ahead
+                ahead = score(other, *jobs[2])
+                absorb(other, state, now, *jobs[1])
+                now = ahead
+                ahead = score(other, *jobs[3])
+                absorb(other, state, now, *jobs[2])
+                now = ahead
+                ahead = score(other, *jobs[4])
+                absorb(other, state, now, *jobs[3])
+                now = ahead
+                ahead = score(other, *jobs[5])
+                absorb(other, state, now, *jobs[4])
+                now = ahead
+                ahead = score(other, *jobs[6])
+                absorb(other, state, now, *jobs[5])
+                now = ahead
+                ahead = score(other, *jobs[7])
+                absorb(other, state, now, *jobs[6])
+                now = ahead
+                absorb(other, state, now, *jobs[7])
 
         @pl.when(n < NBLK)
         def _():
@@ -515,11 +581,11 @@
         def _():
             settle(other, n - 1)
 
-    half(2 * step, 0)
+    half(2 * step, 0, True, True)
 
     @pl.when(step < NBLK // 2)
     def _():
-        half(2 * step + 1, 1)
+        half(2 * step + 1, 1, False, False)
 
     @pl.when(step == NBLK // 2)
     def _():
@@ -534,13 +600,13 @@
         grid=(NBLK // 2 + 1,),
         out_shape=(
             jax.ShapeDtypeStruct((samples, 128, 12, 2, 128), jnp.bfloat16),
-            jax.ShapeDtypeStruct((samples, Q, DL), jnp.float32),
-            jax.ShapeDtypeStruct((samples, Q, 128), jnp.float32),
+            jax.ShapeDtypeStruct((samples, DL, Q), jnp.float32),
+            jax.ShapeDtypeStruct((samples, 8, Q), jnp.float32),
         ),
         in_specs=[whole] * 7,
         out_specs=(pl.BlockSpec(memory_space=pl.ANY), whole, whole),
         scratch_shapes=[
-            pltpu.VMEM((26, KROW, 128), jnp.bfloat16),
+            pltpu.VMEM((2, 26, KROW, 128), jnp.bfloat16),
             pltpu.VMEM((HEADS, DL, Q), jnp.bfloat16),
             pltpu.VMEM((1024, DL), jnp.bfloat16),
             pltpu.VMEM((1024, DL), jnp.bfloat16),
@@ -568,7 +634,7 @@
     feats, weighted, stats = encode(xt, rows, cols, w2, kt, vt, queries)
     features = feats.reshape(samples, 128, lat_rows, lon_cols)
     latents = reduce_all(weighted, stats, out_weight, norm_gain)
-    return (features, latents.reshape(samples, Q, DL))
+    return (features, latents)
 
 
 def solution(mesh):

time: 105 us -> 100 us (0.952)
  Pallas kernels: 101 us -> 95.8 us
    pallas_call x1, Pallas kernels: 29.5 us -> 26.3 us  [reduce_all(): pl.pallas_call(reduce_kernel, out_shape=jax.ShapeDtypeStruct((4, Q, DL),...]
    pallas_call x1, Pallas kernels: 59.1 us -> 57.5 us  [encode(): pl.pallas_call(encode_kernel, grid=(NBLK // 2 + 1,), out_shape=(jax.Shape...]
where the time goes in v4:
time: 100 us
  Pallas kernels  95.8 us (96%)
  local copies, waits for them, and re-layouts  3.65 us (4%)
    pallas_call x1, Pallas kernels, encode(): pl.pallas_call(encode_kernel, grid=(NBLK // 2 + 1,), out_shape=(jax.Shape...  57.5 us
    pallas_call x1, Pallas kernels, reduce_all(): pl.pallas_call(reduce_kernel, out_shape=jax.ShapeDtypeStruct((4, Q, DL),...  26.3 us
    pallas_call x1, Pallas kernels, halo(): pl.pallas_call(halo_kernel, out_shape=(jax.ShapeDtypeStruct((2, samples,...  12 us
    unnamed x12, local copies, waits for them, and re-layouts  3.49 us

profile of v4, /device:TPU:1, one launch (start us, length us, event | category | flops | bytes accessed | tf_op | source)
XLA Modules:
  0.0 100.2 jit_solution(222704025743822548)
XLA Ops:
  0.6 1.7 %copy.10 = bf16[4,69,24,128]{3,1,2,0:T(8,128)(2,1)S(1)} copy(bf16[4,69,24,128]{3,2,1,0:T(8,128)(2,1)} %param.6) | data formatting | bytes 3391488 | tf_op args[0]
  2.3 0.0 copy-start
  2.3 0.0 copy-start.1
  2.4 0.2 pad.4.xt_ref
  2.5 0.7 copy-done
  3.2 0.1 copy-done.1
  3.3 0.0 copy-start.3
  3.3 12.0 %shard_map.77 = (bf16[2,4,80,128]{3,2,1,0:T(8,128)(2,1)S(1)}, bf16[2,4,80,128]{3,2,1,0:T(8,128)(2,1)S(1)}, bf16[256,960]{1,0:T(8,128)(2,1)S(1)}, bf16[256,512]{1,0:T(8,128)(2,1)S(1)}, bf16[512,256]{1,0:T(8,128)(2,1)S(1)}) custom-call(bf16[4,24,80,128]{3,2,1,0:T(8,128)(2,1)S(1)} %pad.4.xt_ref, bf16[9,69,128]{2,1,0:T(8,128)(2,1)S(1)} %bitcast.6, ...), custom_call_target="tpu_custom_call" | custom-call | tf_op jit(solution)/shard_map/pallas_call | solution.py:309
  15.4 0.0 copy-start.2
  15.4 0.0 copy-start.4
  15.4 0.0 copy-done.3
  15.4 57.5 %shard_map.78 = (bf16[4,128,12,2,128]{4,3,2,1,0:T(2,128)(2,1)}, f32[4,256,256]{2,1,0:T(8,128)S(1)}, f32[4,8,256]{2,1,0:T(8,128)S(1)}) custom-call(bf16[4,24,80,128]{3,2,1,0:T(8,128)(2,1)S(1)} %pad.4.xt_ref, bf16[2,4,80,128]{3,2,1,0:T(8,128)(2,1)S(1)} %get-tuple-element.10.rows_ref, bf16[2,4,80,128]{3,2,1,0:T(8,128)(2,1)S(1)} %get-tuple-element.11.cols_ref, ...), custom_call_target="tpu_custom_call" | custom-call | tf_op jit(solution)/shard_map/pallas_call | solution.py:598
  72.9 0.0 copy-done.2
  72.9 0.0 copy-done.4
  72.9 26.3 %shard_map.79 = f32[4,256,256]{2,1,0:T(8,128)S(1)} custom-call(f32[4,256,256]{2,1,0:T(8,128)S(1)} %get-tuple-element.16.w_ref, f32[4,8,256]{2,1,0:T(8,128)S(1)} %get-tuple-element.17.st_ref, bf16[256,256]{1,0:T(8,128)(2,1)S(1)} %copy-done.2, f32[1,256]{1,0:T(1,128)S(1)} %bitcast.7), custom_call_target="tpu_custom_call" | custom-call | tf_op jit(solution)/shard_map/pallas_call | solution.py:137
  99.2 1.0 copy.12
Async XLA Ops:
  2.3 0.9 copy-start
  2.3 1.0 copy-start.1
  3.3 12.1 %copy-start.3 = (bf16[256,256]{1,0:T(8,128)(2,1)S(1)}, bf16[256,256]{1,0:T(8,128)(2,1)}, u32[]{:S(2)}) copy-start(bf16[256,256]{1,0:T(8,128)(2,1)} %q_ref.1) | copy-start | bytes 393220
  15.4 57.5 %copy-start.2 = (bf16[256,256]{1,0:T(8,128)(2,1)S(1)}, bf16[256,256]{1,0:T(8,128)(2,1)}, u32[]{:S(2)}) copy-start(bf16[256,256]{1,0:T(8,128)(2,1)} %ow_ref.1) | copy-start | bytes 393220
  15.4 57.5 %copy-start.4 = (f32[256]{0:T(256)S(1)}, f32[256]{0:T(256)}, u32[]{:S(2)}) copy-start(f32[256]{0:T(256)} %param.10) | copy-start | bytes 3076

commit v5 on v4

--- a/solution.py
+++ b/solution.py
@@ -16,8 +16,8 @@
 
 
 def reduce_kernel(
-    w_ref, st_ref, ow_ref, gain_ref, out_ref,
-    half_w, half_st, msg, recv, gath,
+    w_in, st_in, k_ref, v_ref, q_ref, ow_ref, gain_ref, out_ref,
+    w_ref, st_ref, half_w, half_st, msg, recv, gath,
     sem_a, sem_b, sem_c,
 ):
     lat = lax.axis_index("lat")
@@ -38,6 +38,29 @@
         return 0
 
     lax.fori_loop(1, NCHIP, greet, 0)
+
+    def score(h):
+        return jnp.dot(k_ref[...], q_ref[h], preferred_element_type=jnp.float32)
+
+    tops, totals = [], []
+    ahead = score(0)
+    for h in range(HEADS):
+        s = ahead
+        if h + 1 < HEADS:
+            ahead = score(h + 1)
+        rows = slice(h * HD, (h + 1) * HD)
+        before = st_in[3, h:h + 1]
+        top = jnp.maximum(jnp.max(s, axis=0, keepdims=True), before)
+        p = jnp.exp(s - top)
+        shrink = jnp.exp(before - top)
+        part = jnp.dot(v_ref[rows], p.astype(jnp.bfloat16), preferred_element_type=jnp.float32)
+        w_ref[3, rows] = part + w_in[3, rows] * shrink
+        tops.append(top)
+        totals.append(jnp.sum(p, axis=0, keepdims=True) + st_in[3, 4 + h:5 + h] * shrink)
+    st_ref[3] = jnp.concatenate(tops + totals, axis=0)
+    for i in range(3):
+        w_ref[i] = w_in[i]
+        st_ref[i] = st_in[i]
     pl.semaphore_wait(barrier, NCHIP)
 
     give = 2 - 2 * core
@@ -132,14 +155,16 @@
     pltpu.make_async_copy(size, size, sem_c.at[0]).wait()
 
 
-def reduce_all(weighted, stats, out_weight, norm_gain):
+def reduce_all(weighted, stats, keys, values, turned, out_weight, norm_gain):
     vm = pl.BlockSpec(memory_space=pltpu.VMEM)
     return pl.pallas_call(
         reduce_kernel,
         out_shape=jax.ShapeDtypeStruct((4, Q, DL), jnp.float32),
-        in_specs=[vm] * 4,
+        in_specs=[vm] * 7,
         out_specs=vm,
         scratch_shapes=[
+            pltpu.VMEM((4, DL, Q), jnp.float32),
+            pltpu.VMEM((4, 8, Q), jnp.float32),
             pltpu.VMEM((2, DL, Q), jnp.float32),
             pltpu.VMEM((2, 8, Q), jnp.float32),
             pltpu.VMEM((NCHIP, 2 * ROWS, Q), jnp.bfloat16),
@@ -152,7 +177,7 @@
         compiler_params=pltpu.CompilerParams(
             collective_id=1, has_side_effects=True, vmem_limit_bytes=32 * 1024 * 1024
         ),
-    )(weighted, stats, out_weight, norm_gain.reshape(1, DL))
+    )(weighted, stats, keys, values, turned, out_weight, norm_gain.reshape(1, DL))
 
 
 CP = 80
@@ -334,7 +359,7 @@
 
 
 def encode_kernel(
-    xt_ref, rows_ref, cols_ref, w2_ref, kt_ref, vt_ref, q_ref, feat_ref, w_out, st_out,
+    xt_ref, rows_ref, cols_ref, w2_ref, kt_ref, vt_ref, q_ref, feat_ref, w_out, st_out, k_out, v_out, q_out,
     x3, qs, k_a, k_b, v_a, v_b, feat_a, feat_b, refs, tot, acc, psums, parts, sem,
 ):
     step = pl.program_id(0)
@@ -435,6 +460,15 @@
             tot[h] = jnp.zeros((8, Q), jnp.float32)
             acc[h] = jnp.zeros((HD, Q), jnp.float32)
 
+    def store(b):
+        line = lax.broadcasted_iota(jnp.int32, (8, Q), 0)
+        new = jnp.zeros((8, Q), jnp.float32)
+        for h in range(HEADS):
+            total = jnp.sum(tot[h], axis=0, keepdims=True)
+            new = jnp.where(line == h, refs[h], jnp.where(line == 4 + h, total, new))
+        st_out[b] = new
+        w_out[b] = acc[...].reshape(DL, Q)
+
     def settle(slot, n):
         high = psums[0]
         for h in range(1, HEADS):
@@ -462,21 +496,14 @@
 
         @pl.when(lax.rem(n, 3) == 2)
         def _():
-            b = n // 3
-            line = lax.broadcasted_iota(jnp.int32, (8, Q), 0)
-            new = jnp.zeros((8, Q), jnp.float32)
-            for h in range(HEADS):
-                total = jnp.sum(tot[h], axis=0, keepdims=True)
-                new = jnp.where(line == h, refs[h], jnp.where(line == 4 + h, total, new))
-            st_out[b] = new
-            w_out[b] = acc[...].reshape(DL, Q)
-
-    def half(n, slot, begin, end):
+            store(n // 3)
+
+    def half(n, slot, begin):
         b = n // 3
         c = lax.rem(n, 3)
         other = 1 - slot
 
-        @pl.when(jnp.logical_and(c == 0, n < NBLK))
+        @pl.when(c == 0)
         def _():
             outer_rows(b, lax.rem(b, 2))
 
@@ -538,57 +565,27 @@
             now = ahead
             absorb(other, state, now, *jobs[7])
 
-        if begin or end:
-            pl.when(jnp.logical_and(n > 0, n < NBLK))(mixed)
+        if begin:
+            pl.when(n > 0)(mixed)
         else:
             mixed()
 
-        if end:
-            @pl.when(n == NBLK)
-            def _():
-                jobs = [(h, n) for h in range(HEADS) for n in range(0, 1024, TILE)]
-                ahead = score(other, *jobs[0])
-                state = {}
-                now = ahead
-                ahead = score(other, *jobs[1])
-                absorb(other, state, now, *jobs[0])
-                now = ahead
-                ahead = score(other, *jobs[2])
-                absorb(other, state, now, *jobs[1])
-                now = ahead
-                ahead = score(other, *jobs[3])
-                absorb(other, state, now, *jobs[2])
-                now = ahead
-                ahead = score(other, *jobs[4])
-                absorb(other, state, now, *jobs[3])
-                now = ahead
-                ahead = score(other, *jobs[5])
-                absorb(other, state, now, *jobs[4])
-                now = ahead
-                ahead = score(other, *jobs[6])
-                absorb(other, state, now, *jobs[5])
-                now = ahead
-                ahead = score(other, *jobs[7])
-                absorb(other, state, now, *jobs[6])
-                now = ahead
-                absorb(other, state, now, *jobs[7])
-
-        @pl.when(n < NBLK)
-        def _():
-            out_copy(n, slot).start()
+        out_copy(n, slot).start()
 
         @pl.when(n > 0)
         def _():
             settle(other, n - 1)
 
-    half(2 * step, 0, True, True)
-
-    @pl.when(step < NBLK // 2)
-    def _():
-        half(2 * step + 1, 1, False, False)
-
-    @pl.when(step == NBLK // 2)
-    def _():
+    half(2 * step, 0, True)
+    half(2 * step + 1, 1, False)
+
+    @pl.when(step == NBLK // 2 - 1)
+    def _():
+        store(xt_ref.shape[0] - 1)
+        k_out[...] = ks[1][...]
+        v_out[...] = vs[1][...]
+        q_out[...] = qs[...]
+        out_copy(NBLK - 2, 0).wait()
         out_copy(NBLK - 1, 1).wait()
 
 
@@ -597,14 +594,17 @@
     whole = pl.BlockSpec(memory_space=pltpu.VMEM)
     return pl.pallas_call(
         encode_kernel,
-        grid=(NBLK // 2 + 1,),
+        grid=(NBLK // 2,),
         out_shape=(
             jax.ShapeDtypeStruct((samples, 128, 12, 2, 128), jnp.bfloat16),
             jax.ShapeDtypeStruct((samples, DL, Q), jnp.float32),
             jax.ShapeDtypeStruct((samples, 8, Q), jnp.float32),
+            jax.ShapeDtypeStruct((1024, DL), jnp.bfloat16),
+            jax.ShapeDtypeStruct((DL, 1024), jnp.bfloat16),
+            jax.ShapeDtypeStruct((HEADS, DL, Q), jnp.bfloat16),
         ),
         in_specs=[whole] * 7,
-        out_specs=(pl.BlockSpec(memory_space=pl.ANY), whole, whole),
+        out_specs=(pl.BlockSpec(memory_space=pl.ANY),) + (whole,) * 5,
         scratch_shapes=[
             pltpu.VMEM((2, 26, KROW, 128), jnp.bfloat16),
             pltpu.VMEM((HEADS, DL, Q), jnp.bfloat16),
@@ -631,9 +631,9 @@
     xt = jnp.pad(jnp.transpose(fields, (0, 2, 1, 3)), ((0, 0), (0, 0), (0, CP - channels), (0, 0)))
     conv_t = jnp.transpose(conv_weight, (0, 2, 1))
     rows, cols, w2, kt, vt = halo(xt, conv_t, kv_weight)
-    feats, weighted, stats = encode(xt, rows, cols, w2, kt, vt, queries)
+    feats, weighted, stats, keys, values, turned = encode(xt, rows, cols, w2, kt, vt, queries)
     features = feats.reshape(samples, 128, lat_rows, lon_cols)
-    latents = reduce_all(weighted, stats, out_weight, norm_gain)
+    latents = reduce_all(weighted, stats, keys, values, turned, out_weight, norm_gain)
     return (features, latents)
 
 

time: 100 us -> 96.3 us (0.963)
  Pallas kernels: 95.8 us -> 91.8 us
    pallas_call x1, Pallas kernels: 57.5 us -> 53.5 us  [encode(): pl.pallas_call(encode_kernel, grid=(NBLK // 2,), out_shape=(jax.ShapeDtyp...]
where the time goes in v5:
time: 96.3 us; the launch traced here: 96.2 us
  Pallas kernels  91.8 us (95%)
  local copies, waits for them, and re-layouts  3.65 us (4%)
    pallas_call x1, Pallas kernels, encode(): pl.pallas_call(encode_kernel, grid=(NBLK // 2,), out_shape=(jax.ShapeDtyp...  53.5 us
    pallas_call x1, Pallas kernels, reduce_all(): pl.pallas_call(reduce_kernel, out_shape=jax.ShapeDtypeStruct((4, Q, DL),...  26.3 us
    pallas_call x1, Pallas kernels, halo(): pl.pallas_call(halo_kernel, out_shape=(jax.ShapeDtypeStruct((2, samples,...  12 us
    unnamed x12, local copies, waits for them, and re-layouts  3.49 us

profile of v5, /device:TPU:1, one launch (start us, length us, event | category | flops | bytes accessed | tf_op | source)
XLA Modules:
  0.0 96.2 jit_solution(11245179174365537471)
XLA Ops:
  0.6 1.7 %copy.10 = bf16[4,69,24,128]{3,1,2,0:T(8,128)(2,1)S(1)} copy(bf16[4,69,24,128]{3,2,1,0:T(8,128)(2,1)} %param.6) | data formatting | bytes 3391488 | tf_op args[0]
  2.3 0.0 copy-start
  2.3 0.0 copy-start.1
  2.4 0.2 pad.4.xt_ref
  2.5 0.7 copy-done
  3.2 0.1 copy-done.1
  3.3 0.0 copy-start.3
  3.3 12.0 %shard_map.77 = (bf16[2,4,80,128]{3,2,1,0:T(8,128)(2,1)S(1)}, bf16[2,4,80,128]{3,2,1,0:T(8,128)(2,1)S(1)}, bf16[256,960]{1,0:T(8,128)(2,1)S(1)}, bf16[256,512]{1,0:T(8,128)(2,1)S(1)}, bf16[512,256]{1,0:T(8,128)(2,1)S(1)}) custom-call(bf16[4,24,80,128]{3,2,1,0:T(8,128)(2,1)S(1)} %pad.4.xt_ref, bf16[9,69,128]{2,1,0:T(8,128)(2,1)S(1)} %bitcast.6, ...), custom_call_target="tpu_custom_call" | custom-call | tf_op jit(solution)/shard_map/pallas_call | solution.py:334
  15.4 0.0 copy-start.2
  15.4 0.0 copy-start.4
  15.4 0.0 copy-done.3
  15.4 53.5 %shard_map.78 = (bf16[4,128,12,2,128]{4,3,2,1,0:T(2,128)(2,1)}, f32[4,256,256]{2,1,0:T(8,128)S(1)}, f32[4,8,256]{2,1,0:T(8,128)S(1)}, bf16[1024,256]{1,0:T(8,128...) custom-call(bf16[4,24,80,128]{3,2,1,0:T(8,128)(2,1)S(1)} %pad.4.xt_ref, ...), custom_call_target="tpu_custom_call" | custom-call | tf_op jit(solution)/shard_map/pallas_call | solution.py:595
  68.9 0.0 copy-done.2
  68.9 0.0 copy-done.4
  69.0 26.3 %shard_map.79 = f32[4,256,256]{2,1,0:T(8,128)S(1)} custom-call(f32[4,256,256]{2,1,0:T(8,128)S(1)} %get-tuple-element.19.w_in, f32[4,8,256]{2,1,0:T(8,128)S(1)} %get-tuple-element.20.st_in, bf16[1024,256]{1,0:T(8,128)(2,1)S(1)} %get-tuple-element.21.k_ref, bf16[256,1024]{1,0:T(8,128)(2,1)S(1)} %get-tuple-element.22.v_ref, ...), custom_call_target="tpu_custom_call" | custom-call | tf_op jit(solution)/shard_map/pallas_call | solution.py:160
  95.2 1.0 %copy.12 = f32[4,256,256]{2,1,0:T(8,128)} copy(f32[4,256,256]{2,1,0:T(8,128)S(1)} %shard_map.79) | data formatting | bytes 2097152
Async XLA Ops:
  2.3 0.9 copy-start
  2.3 1.0 %copy-start.1 = (bf16[512,128]{1,0:T(8,128)(2,1)S(1)}, bf16[512,128]{1,0:T(8,128)(2,1)}, u32[]{:S(2)}) copy-start(bf16[512,128]{1,0:T(8,128)(2,1)} %kv_ref.1) | copy-start | bytes 393220
  3.3 12.1 %copy-start.3 = (bf16[256,256]{1,0:T(8,128)(2,1)S(1)}, bf16[256,256]{1,0:T(8,128)(2,1)}, u32[]{:S(2)}) copy-start(bf16[256,256]{1,0:T(8,128)(2,1)} %q_ref.1) | copy-start | bytes 393220
  15.4 53.6 %copy-start.2 = (bf16[256,256]{1,0:T(8,128)(2,1)S(1)}, bf16[256,256]{1,0:T(8,128)(2,1)}, u32[]{:S(2)}) copy-start(bf16[256,256]{1,0:T(8,128)(2,1)} %ow_ref.1) | copy-start | bytes 393220
  15.4 53.6 %copy-start.4 = (f32[256]{0:T(256)S(1)}, f32[256]{0:T(256)}, u32[]{:S(2)}) copy-start(f32[256]{0:T(256)} %param.10) | copy-start | bytes 3076

commit v6 on v5

--- a/solution.py
+++ b/solution.py
@@ -518,11 +518,12 @@
         if begin:
             @pl.when(n == 0)
             def _():
-                for part in range(3):
-                    inner_rows(0, 0, part)
-                inner_rows(1, 1, 0)
+                inner_rows(0, 0, 0)
+                inner_rows(0, 0, 1)
                 f0 = conv_of(b, c, 0)
                 f1 = conv_of(b, c, 1)
+                inner_rows(0, 0, 2)
+                inner_rows(1, 1, 0)
                 keep_features(f0, slot, 0)
                 project(f0, slot, 0)
                 keep_features(f1, slot, 1)

time: 96.3 us -> 96.7 us (level)
  no operation moved by 1% of the time
where the time goes in v6:
time: 96.7 us; the launch traced here: 96.5 us
  Pallas kernels  92.1 us (95%)
  local copies, waits for them, and re-layouts  3.65 us (4%)
    pallas_call x1, Pallas kernels, encode(): pl.pallas_call(encode_kernel, grid=(NBLK // 2,), out_shape=(jax.ShapeDtyp...  53.3 us
    pallas_call x1, Pallas kernels, reduce_all(): pl.pallas_call(reduce_kernel, out_shape=jax.ShapeDtypeStruct((4, Q, DL),...  26.8 us
    pallas_call x1, Pallas kernels, halo(): pl.pallas_call(halo_kernel, out_shape=(jax.ShapeDtypeStruct((2, samples,...  12 us
    unnamed x12, local copies, waits for them, and re-layouts  3.49 us

profile of v6, /device:TPU:1, one launch (start us, length us, event | category | flops | bytes accessed | tf_op | source)
XLA Modules:
  0.0 96.5 jit_solution(1528961978624276326)
XLA Ops:
  0.6 1.7 %copy.10 = bf16[4,69,24,128]{3,1,2,0:T(8,128)(2,1)S(1)} copy(bf16[4,69,24,128]{3,2,1,0:T(8,128)(2,1)} %param.6) | data formatting | bytes 3391488 | tf_op args[0]
  2.3 0.0 copy-start
  2.3 0.0 copy-start.1
  2.4 0.2 pad.4.xt_ref
  2.5 0.7 copy-done
  3.2 0.1 copy-done.1
  3.3 0.0 copy-start.3
  3.3 12.0 %shard_map.77 = (bf16[2,4,80,128]{3,2,1,0:T(8,128)(2,1)S(1)}, bf16[2,4,80,128]{3,2,1,0:T(8,128)(2,1)S(1)}, bf16[256,960]{1,0:T(8,128)(2,1)S(1)}, bf16[256,512]{1,0:T(8,128)(2,1)S(1)}, bf16[512,256]{1,0:T(8,128)(2,1)S(1)}) custom-call(bf16[4,24,80,128]{3,2,1,0:T(8,128)(2,1)S(1)} %pad.4.xt_ref, bf16[9,69,128]{2,1,0:T(8,128)(2,1)S(1)} %bitcast.6, ...), custom_call_target="tpu_custom_call" | custom-call | tf_op jit(solution)/shard_map/pallas_call | solution.py:334
  15.4 0.0 copy-start.2
  15.4 0.0 copy-start.4
  15.4 0.0 copy-done.3
  15.4 53.3 %shard_map.78 = (bf16[4,128,12,2,128]{4,3,2,1,0:T(2,128)(2,1)}, f32[4,256,256]{2,1,0:T(8,128)S(1)}, f32[4,8,256]{2,1,0:T(8,128)S(1)}, bf16[1024,256]{1,0:T(8,128...) custom-call(bf16[4,24,80,128]{3,2,1,0:T(8,128)(2,1)S(1)} %pad.4.xt_ref, ...), custom_call_target="tpu_custom_call" | custom-call | tf_op jit(solution)/shard_map/pallas_call | solution.py:596
  68.7 0.0 copy-done.2
  68.7 0.0 copy-done.4
  68.7 26.8 %shard_map.79 = f32[4,256,256]{2,1,0:T(8,128)S(1)} custom-call(f32[4,256,256]{2,1,0:T(8,128)S(1)} %get-tuple-element.19.w_in, f32[4,8,256]{2,1,0:T(8,128)S(1)} %get-tuple-element.20.st_in, bf16[1024,256]{1,0:T(8,128)(2,1)S(1)} %get-tuple-element.21.k_ref, bf16[256,1024]{1,0:T(8,128)(2,1)S(1)} %get-tuple-element.22.v_ref, ...), custom_call_target="tpu_custom_call" | custom-call | tf_op jit(solution)/shard_map/pallas_call | solution.py:160
  95.5 1.0 %copy.12 = f32[4,256,256]{2,1,0:T(8,128)} copy(f32[4,256,256]{2,1,0:T(8,128)S(1)} %shard_map.79) | data formatting | bytes 2097152
Async XLA Ops:
  2.3 0.9 copy-start
  2.3 1.0 %copy-start.1 = (bf16[512,128]{1,0:T(8,128)(2,1)S(1)}, bf16[512,128]{1,0:T(8,128)(2,1)}, u32[]{:S(2)}) copy-start(bf16[512,128]{1,0:T(8,128)(2,1)} %kv_ref.1) | copy-start | bytes 393220
  3.3 12.1 %copy-start.3 = (bf16[256,256]{1,0:T(8,128)(2,1)S(1)}, bf16[256,256]{1,0:T(8,128)(2,1)}, u32[]{:S(2)}) copy-start(bf16[256,256]{1,0:T(8,128)(2,1)} %q_ref.1) | copy-start | bytes 393220
  15.4 53.3 %copy-start.2 = (bf16[256,256]{1,0:T(8,128)(2,1)S(1)}, bf16[256,256]{1,0:T(8,128)(2,1)}, u32[]{:S(2)}) copy-start(bf16[256,256]{1,0:T(8,128)(2,1)} %ow_ref.1) | copy-start | bytes 393220
  15.4 53.3 %copy-start.4 = (f32[256]{0:T(256)S(1)}, f32[256]{0:T(256)}, u32[]{:S(2)}) copy-start(f32[256]{0:T(256)} %param.10) | copy-start | bytes 3076
